TPU v7x, 256 devices: a whole 4x4x8 slice. The times are simulated.
256 devices in a mesh: group: 8 (over z), dev: 32 (over y, x, core).
Axes of the slice: x: 4, y: 4, z: 8, core: 2. Of those that a mesh axis runs over, the one named last changes fastest.
Arguments:
- features: bfloat16 [1536, 64, 512], P(('group', 'dev')), may hold values from -6 to 6
- cotangent: bfloat16 [1536, 64, 512], P(('group', 'dev')), may hold values from -0.03125 to 0.03125
- first_weight: bfloat16 [64, 27, 64], replicated, may hold values from -0.15625 to 0.15625
- second_weight: bfloat16 [64, 27, 64], replicated, may hold values from -0.15625 to 0.15625
- counts: int32 [8, 32], replicated, may hold values from 0 to 6, as said below
- neighbours: int32 [1536, 26], P(('group', 'dev')), may hold values from -1 to 1535, as said below
Outputs:
- blocks_out: bfloat16 [1536, 64, 512], P(('group', 'dev'))
- first_grad: float32 [64, 27, 64], replicated
- second_grad: float32 [64, 27, 64], replicated
Inputs may be any that keep to these rules, and one draw needn't show every extreme that they name: `counts`: slots 0 to count - 1 of a device hold its bricks. The bricks of group g form one layer of the scene, 64 of them, taken along a Morton curve of the layer and cut into consecutive ranges, device after device. In every group some device holds 6 bricks. A live brick's entries name live bricks only; free slots hold -1 in every direction. A brick of group g has neighbours only in groups g + dz. The relation is symmetric: if s names r in direction k, r names s in the opposite direction.
All inputs are finite; a program needn't handle non-finite values.
Results may differ from a plain program's by a relative error of at most 0.005.
Values may be sent and summed in bfloat16 or wider, within the bound.
A program may use at most 128 MiB of HBM per device.

v0:
```python
import jax
import jax.numpy as jnp
import numpy as np
from jax import lax
from jax.sharding import PartitionSpec as P


def from_behind(value, axis, steps):
    count = lax.axis_size(axis)
    first, last = (max(0, -steps), min(count, count - steps))
    return lax.ppermute(value, axis, [(source, source + steps) for source in range(first, last)])


def cube_tables():
    face_index = []
    for face_id in range(6):
        for outer in range(8):
            for inner in range(8):
                edge_value = 0 if face_id % 2 == 0 else 7
                if face_id < 2:
                    face_index.append(outer * 64 + inner * 8 + edge_value)
                elif face_id < 4:
                    face_index.append(outer * 64 + edge_value * 8 + inner)
                else:
                    face_index.append(edge_value * 64 + outer * 8 + inner)
    directions = []
    for step_z in (-1, 0, 1):
        for step_y in (-1, 0, 1):
            for step_x in (-1, 0, 1):
                if step_z != 0 or step_y != 0 or step_x != 0:
                    directions.append((step_z, step_y, step_x))
    halo_direction = []
    halo_column = []
    cube_order = []
    for placement_depth in range(-1, 9):
        for place_y in range(-1, 9):
            for place_x in range(-1, 9):
                if 0 <= placement_depth < 8 and 0 <= place_y < 8 and (0 <= place_x < 8):
                    cube_order.append(placement_depth * 64 + place_y * 8 + place_x)
                    continue
                step_z = -1 if placement_depth < 0 else 1 if placement_depth > 7 else 0
                step_y = -1 if place_y < 0 else 1 if place_y > 7 else 0
                step_x = -1 if place_x < 0 else 1 if place_x > 7 else 0
                other_z = placement_depth - 8 * step_z
                other_y = place_y - 8 * step_y
                other_x = place_x - 8 * step_x
                if step_z != 0:
                    face_id = 4 if step_z == 1 else 5
                    within = other_y * 8 + other_x
                elif step_x != 0:
                    face_id = 0 if step_x == 1 else 1
                    within = other_z * 8 + other_y
                else:
                    face_id = 2 if step_y == 1 else 3
                    within = other_z * 8 + other_x
                halo_direction.append(directions.index((step_z, step_y, step_x)))
                halo_column.append(face_id * 64 + within)
                cube_order.append(512 + len(halo_column) - 1)
    return (
        np.array(face_index, np.int32),
        np.array(halo_direction, np.int32),
        np.array(halo_column, np.int32),
        np.array(cube_order, np.int32),
    )


def shifted_layer(layer, steps):
    channels, slots = (layer.shape[0], layer.shape[1])
    moved = from_behind(layer.reshape(channels, slots * 64), "group", steps)
    return moved.reshape(channels, slots, 64)


def build_cubes(bricks, neighbours):
    slots, channels = (bricks.shape[0], bricks.shape[1])
    face_index, halo_direction, halo_column, cube_order = cube_tables()
    faces = jnp.transpose(jnp.take(bricks, jnp.asarray(face_index), axis=2), (1, 0, 2))
    from_above = shifted_layer(faces[:, :, 256:320], -1)
    from_below = shifted_layer(faces[:, :, 320:384], 1)
    block = jnp.concatenate([faces[:, :, :256], from_above, from_below], axis=2).reshape(
        channels, slots * 384
    )
    device_count = lax.axis_size("dev")
    chosen = neighbours[:, jnp.asarray(halo_direction)]
    valid = chosen >= 0
    safe = jnp.maximum(chosen, 0)
    columns = (
        (safe // slots % device_count * slots + safe % slots) * 384
        + jnp.asarray(halo_column)[None, :]
    ).reshape(-1)
    valid_flat = valid.reshape(-1)
    empty = jnp.zeros((channels, slots * 488), jnp.bfloat16)
    piece = lax.all_gather(block, "dev", axis=1, tiled=True)
    width = piece.shape[1]
    offset_cols = columns - jnp.int32(0)
    usable = valid_flat & (offset_cols >= 0) & (offset_cols < width)
    picked = jnp.take(piece, jnp.clip(offset_cols, 0, width - 1), axis=1)
    halo = jnp.where(usable[None, :], picked, empty)
    halo = jnp.transpose(halo.reshape(channels, slots, 488), (1, 0, 2))
    cube = jnp.concatenate([bricks, halo], axis=2)
    return jnp.take(cube, jnp.asarray(cube_order), axis=2)


def convolve(brick_cubes, weight):
    slots, channels = (brick_cubes.shape[0], brick_cubes.shape[1])
    outputs = weight.shape[0]
    grid = brick_cubes.reshape(slots, channels, 10, 10, 10)
    kernel = jnp.transpose(weight.reshape(outputs, 3, 3, 3, weight.shape[2]), (0, 4, 1, 2, 3))
    result = lax.conv_general_dilated(
        grid,
        kernel,
        (1, 1, 1),
        "VALID",
        dimension_numbers=("NCDHW", "OIDHW", "NCDHW"),
        preferred_element_type=jnp.float32,
    )
    return result.reshape(slots, outputs, 512)


def weight_gradient(gradient_list, brick_cubes):
    slots, channels = (brick_cubes.shape[0], brick_cubes.shape[1])
    outputs = gradient_list.shape[1]
    grid = brick_cubes.reshape(slots, channels, 10, 10, 10)
    grads = gradient_list.reshape(slots, outputs, 8, 8, 8)
    result = lax.conv_general_dilated(
        grid,
        grads,
        (1, 1, 1),
        "VALID",
        dimension_numbers=("CNDHW", "IODHW", "NCDHW"),
        preferred_element_type=jnp.float32,
    )
    return jnp.transpose(result, (1, 2, 3, 4, 0)).reshape(outputs, 27 * channels)


def residual_block(bricks, cotangent, neighbours, live, first_weight, second_weight):
    live_mask = live[:, None, None]
    x_cubes = build_cubes(bricks, neighbours)
    first = convolve(x_cubes, first_weight)
    hidden = jnp.where(live_mask, jnp.maximum(first, 0.0), 0.0).astype(jnp.bfloat16)
    h_cubes = build_cubes(hidden, neighbours)
    second = convolve(h_cubes, second_weight)
    output = jnp.where(live_mask, bricks.astype(jnp.float32) + second, 0.0).astype(jnp.bfloat16)
    upstream = jnp.where(live_mask, cotangent, jnp.zeros_like(cotangent))
    second_grad = weight_gradient(upstream, h_cubes)
    g_cubes = build_cubes(upstream, neighbours)
    flipped = jnp.transpose(second_weight[:, ::-1, :], (2, 1, 0))
    back = convolve(g_cubes, flipped)
    hidden_grad = jnp.where(hidden > 0, back, 0.0).astype(jnp.bfloat16)
    first_grad = weight_gradient(hidden_grad, x_cubes)
    first_grad, second_grad = lax.psum((first_grad, second_grad), ("group", "dev"))
    return (
        output,
        first_grad.reshape(first_weight.shape),
        second_grad.reshape(second_weight.shape),
    )


def per_device(features, cotangent, first_weight, second_weight, counts, neighbours):
    cap = features.shape[0]
    group_index = lax.axis_index("group")
    device_index = lax.axis_index("dev")
    slot_ids = jnp.arange(cap, dtype=jnp.int32)
    alive = slot_ids < counts[group_index, device_index]
    output, first_grad, second_grad = residual_block(
        features, cotangent, neighbours, alive, first_weight, second_weight
    )
    return (output, first_grad, second_grad)


def solution(mesh):
    placed = (
        P(("group", "dev"), None, None),
        P(("group", "dev"), None, None),
        P(),
        P(),
        P(),
        P(("group", "dev"), None),
    )
    return jax.shard_map(
        per_device,
        mesh=mesh,
        in_specs=placed,
        out_specs=(P(("group", "dev"), None, None), P(), P()),
        check_vma=False,
    )
```

profile of v0, /device:TPU:1, one launch (start us, length us, event | category | flops | bytes accessed | tf_op | source)
XLA Modules:
  0.0 663.6 jit_solution(14973791488448514991)
XLA Ops:
  7.2 0.7 pad_clamp_fusion.2
  8.0 1.8 copy.179
  9.7 1.7 gather_fusion.1
  11.8 1.3 collective-permute-start
  13.5 5.0 collective-permute-start.1
  18.9 0.8 collective-permute-done.1
  20.2 0.9 copy.212
  21.3 1.2 gather_fusion
  23.1 1.7 copy.199
  24.8 1.3 dynamic_slice.3
  26.1 1.1 iota_compare_fusion
  27.3 82.5 %all-gather.4.cloned.1.call-done = bf16[64,73728]{0,1:T(8,128)(2,1)} async-done(((bf16[64,2304]{0,1:T(8,128)(2,1)}), bf16[64,73728]{0,1:T(8,128)(2,1)}) %all-gather.4.cloned.1.call-update) | async-done | bytes 9437200 | tf_op jit(solution)/shard_map/all_gather | solution.py:92
  109.8 14.0 %gather_fusion.2 = bf16[2928,64]{1,0:T(8,128)(2,1)S(1)} fusion(bf16[64,73728]{0,1:T(8,128)(2,1)} %all-gather.4.cloned.1.call-done, s32[3072]{0:T(1024)S(1)} %pad_clamp_fusion), kind=kCustom, calls=%fused_computation.1.clone | custom fusion | bytes 761280 | tf_op jit(solution)/shard_map/jit(_take)/gather | solution.py:96
  123.8 1.9 bitcast_select_fusion.3
  126.1 1.0 pad_maximum_fusion.3
  127.1 3.1 copy.191
  130.2 7.7 %gather_fusion.3 = bf16[1000,6,64]{2,1,0:T(8,128)(2,1)} fusion(bf16[6,64,1000]{1,0,2:T(8,128)(2,1)S(1)} %copy.191, s32[1024]{0:T(1024)S(1)} %pad_clamp_fusion.1), kind=kCustom, calls=%fused_computation.2.clone | custom fusion | bytes 1540000 | tf_op jit(solution)/shard_map/jit(_take)/gather | solution.py:100
  137.9 11.0 %fusion.3 = (u8[6,64,8,8]{1,0,3,2:T(8,128)(4,1)}, bf16[6,64,8,8,8]{1,0,4,3,2:T(8,128)(2,1)S(1)}) fusion(pred[6]{0:T(512)(128)(4,1)} %iota_compare_fusion, bf16[6,64,10,10,10]{1,0,4,3,2:T(8,128)(2,1)} %bitcast.96, bf16[64,3,3,3,64]{4,0,3,2,1:T(8,128)(2,1)S(1)} %bitcast.75), kind=kOutput, calls=%fused_computation.32 | convolution fusion | flops 681418752 | bytes 1406982 | tf_op jit(solution)/shard_map/conv_general_dilated | solution.py:108
  148.9 1.5 broadcast_select_fusion
  150.4 2.2 gather_fusion.4
  153.0 1.3 collective-permute-start.2
  154.6 4.0 collective-permute-start.3
  158.6 1.1 slice.59
  160.6 0.9 copy.213
  161.6 2.0 gather_fusion.7
  163.9 1.3 collective-permute-start.4
  165.5 4.6 collective-permute-start.5
  170.1 1.1 slice.62
  171.6 1.0 reshape.328
  173.0 0.9 copy.214
  174.0 0.8 rev.3
  174.8 71.8 %all-gather.6.cloned.1.call-done = bf16[64,73728]{0,1:T(8,128)(2,1)} async-done(((bf16[64,2304]{0,1:T(8,128)(2,1)}), bf16[64,73728]{0,1:T(8,128)(2,1)}) %all-gather.6.cloned.1.call-update) | async-done | bytes 9437200 | tf_op jit(solution)/shard_map/all_gather | solution.py:92
  246.6 14.0 %gather_fusion.5 = bf16[2928,64]{1,0:T(8,128)(2,1)S(1)} fusion(bf16[64,73728]{0,1:T(8,128)(2,1)} %all-gather.6.cloned.1.call-done, s32[3072]{0:T(1024)S(1)} %pad_clamp_fusion), kind=kCustom, calls=%fused_computation.5.clone | custom fusion | bytes 761280 | tf_op jit(solution)/shard_map/jit(_take)/gather | solution.py:96
  260.7 71.2 %all-gather.8.cloned.1.call-done = bf16[64,73728]{0,1:T(8,128)(2,1)} async-done(((bf16[64,2304]{0,1:T(8,128)(2,1)}), bf16[64,73728]{0,1:T(8,128)(2,1)}) %all-gather.8.cloned.1.call-update) | async-done | bytes 9437200 | tf_op jit(solution)/shard_map/all_gather | solution.py:92
  331.9 15.3 %gather_fusion.8 = bf16[2928,64]{1,0:T(8,128)(2,1)} fusion(bf16[64,73728]{0,1:T(8,128)(2,1)} %all-gather.8.cloned.1.call-done, s32[3072]{0:T(1024)S(1)} %pad_clamp_fusion), kind=kCustom, calls=%fused_computation.6.clone | custom fusion | bytes 761280 | tf_op jit(solution)/shard_map/jit(_take)/gather | solution.py:96
  347.2 3.4 bitcast_select_fusion.1
  351.0 0.8 copy-done.2
  351.8 3.0 pad_maximum_fusion
  354.8 9.2 %gather_fusion.6 = bf16[1000,6,64]{2,1,0:T(8,128)(2,1)} fusion(bf16[6,64,1000]{1,0,2:T(8,128)(2,1)} %get-tuple-element.41, s32[1024]{0:T(1024)S(1)} %pad_clamp_fusion.1), kind=kCustom, calls=%fused_computation.7.clone | custom fusion | bytes 1540000 | tf_op jit(solution)/shard_map/jit(_take)/gather | solution.py:100
  364.1 9.6 %gather_fusion.9 = bf16[1000,6,64]{2,1,0:T(8,128)(2,1)} fusion(bf16[6,64,1000]{1,0,2:T(8,128)(2,1)} %get-tuple-element.42, s32[1024]{0:T(1024)S(1)} %pad_clamp_fusion.1), kind=kCustom, calls=%fused_computation.8.clone | custom fusion | bytes 1540000 | tf_op jit(solution)/shard_map/jit(_take)/gather | solution.py:100
  373.7 6.6 fusion.18
  380.3 15.1 %fusion.4 = f32[64,3,3,3,64]{4,0,3,2,1:T(8,128)} fusion(bf16[6,64,10,10,10]{1,0,4,3,2:T(8,128)(2,1)} %bitcast.97, bf16[6,64,10,10,10]{1,0,4,3,2:T(8,128)(2,1)} %bitcast.100, bf16[64,3,3,3,64]{0,4,3,2,1:T(8,128)(2,1)S(1)} %bitcast.95, u8[6,64,8,8]{1,0,3,2:T(8,128)(4,1)S(1)} %copy-done.23), kind=kOutput, calls=%fused_computation.33 | convolution fusion | flops 1360134144 | bytes 2224128 | tf_op jit(solution)/shard_map/transpose | solution.py:132
  395.5 10.3 %fusion.17 = f32[6,64,8,8,8]{1,0,4,3,2:T(8,128)S(1)} fusion(bf16[6,64,10,10,10]{1,0,4,3,2:T(8,128)(2,1)} %bitcast.99, bf16[64,3,3,3,64]{4,0,3,2,1:T(8,128)(2,1)S(1)} %bitcast.94), kind=kOutput, calls=%fused_computation.62 | convolution fusion | flops 679477248 | bytes 1775616 | tf_op jit(solution)/shard_map/conv_general_dilated | solution.py:108
  405.8 0.5 fusion.1
  406.3 1.4 copy.211
  407.6 246.1 %all-reduce.3.cloned.1.call-done = (f32[64,27,64]{2,0,1:T(8,128)}, f32[64,27,64]{2,0,1:T(8,128)}) async-done(((f32[64,27,64]{2,0,1:T(8,128)}, f32[64,27,64]{2,0,1:T(8,128)}), (f32[64,27,64]{2,0,1:T(8,128)}, f32[64,27,64]{2,0,1:T(8,128)})) %all-reduce.3.cloned.1.call-update) | async-done | bytes 884752 | tf_op jit(solution)/shard_map/psum | solution.py:150
  653.8 2.3 copy.225
  656.0 0.9 copy.226
  (109 shorter events, 6.1 us)
Async XLA Ops:
  7.2 130.7 %copy-start = (bf16[64,27,64]{2,0,1:T(8,128)(2,1)S(1)}, bf16[64,27,64]{2,0,1:T(8,128)(2,1)}, u32[]{:S(2)}) copy-start(bf16[64,27,64]{2,0,1:T(8,128)(2,1)} %param.26) | copy-start | bytes 663556
  7.2 102.6 %all-gather.4.cloned.1.call-start = ((), (), s32[]{:S(2)}) async-start(), calls=%async_computation | async-start | bytes 19464192 | tf_op jit(solution)/shard_map/all_gather | solution.py:92
  8.0 3.6 copy-start.16
  11.8 6.7 %collective-permute-start = (bf16[64,384]{1,0:T(8,128)(2,1)S(1)}, bf16[64,384]{1,0:T(8,128)(2,1)S(1)}, u32[]{:S(2)}, u32[]{:S(2)}) collective-permute-start(bf16[64,384]{1,0:T(8,128)(2,1)S(1)} %reshape.308), channel_id=1, source_target_pairs={{32,0},{64,32},{96,64},{128,96},{160,128},{192,160},{224,192},{33,... | collective-permute-start | bytes 147464 | tf_op jit(solution)/shard_map/ppermute | solution.py:11
  13.5 6.2 collective-permute-start.1
  18.8 2.4 copy-start.18
  18.8 2.4 copy-start.22
  19.9 3.1 copy-start.21
  19.9 3.2 copy-start.11
  20.2 7.0 %copy-start.19 = (s32[1000]{0:T(1024)S(1)}, s32[1000]{0:T(1024)}, u32[]{:S(2)}) copy-start(s32[1000]{0:T(1024)} %constant.194) | copy-start | bytes 12004
  21.1 225.5 %all-gather.6.cloned.1.call-start = ((), (), s32[]{:S(2)}) async-start(), calls=%async_computation.1 | async-start | bytes 19464192 | tf_op jit(solution)/shard_map/all_gather | solution.py:92
  27.2 98.5 %copy-start.12 = (pred[2928]{0:T(1024)(128)(4,1)}, pred[2928]{0:T(1024)(128)(4,1)S(1)}, u32[]{:S(2)}) copy-start(pred[2928]{0:T(1024)(128)(4,1)S(1)} %get-tuple-element.23) | copy-start | bytes 8788
  27.3 98.5 %copy-start.14 = (pred[2928]{0:T(1024)(128)(4,1)}, pred[2928]{0:T(1024)(128)(4,1)S(1)}, u32[]{:S(2)}) copy-start(pred[2928]{0:T(1024)(128)(4,1)S(1)} %compare_and_fusion) | copy-start | bytes 8788
  123.8 2.3 copy-start.4
  137.9 11.0 %copy-start.3 = (bf16[6,64,512]{1,0,2:T(8,128)(2,1)S(1)}, bf16[6,64,512]{1,0,2:T(8,128)(2,1)}, u32[]{:S(2)}) copy-start(bf16[6,64,512]{1,0,2:T(8,128)(2,1)} %copy.199) | copy-start | bytes 1179652
  137.9 11.0 %copy-start.20 = (pred[6]{0:T(512)(128)(4,1)S(1)}, pred[6]{0:T(512)(128)(4,1)}, u32[]{:S(2)}) copy-start(pred[6]{0:T(512)(128)(4,1)} %iota_compare_fusion) | copy-start | bytes 22
  148.9 1.5 copy-start.17
  152.7 2.0 copy-start.6
  153.0 6.8 %collective-permute-start.2 = (bf16[64,384]{1,0:T(8,128)(2,1)S(1)}, bf16[64,384]{1,0:T(8,128)(2,1)S(1)}, u32[]{:S(2)}, u32[]{:S(2)}) collective-permute-start(bf16[64,384]{1,0:T(8,128)(2,1)S(1)} %reshape.316), channel_id=1, source_target_pairs={{32,0},{64,32},{96,64},{128,96},{160,128},{192,160},{224,192},{33,... | collective-permute-start | bytes 147464 | tf_op jit(solution)/shard_map/ppermute | solution.py:11
  154.6 5.5 collective-permute-start.3
  161.6 170.3 %all-gather.8.cloned.1.call-start = ((), (), s32[]{:S(2)}) async-start(), calls=%async_computation.2 | async-start | bytes 19464192 | tf_op jit(solution)/shard_map/all_gather | solution.py:92
  163.6 2.0 copy-start.5
  163.9 7.4 %collective-permute-start.4 = (bf16[64,384]{1,0:T(8,128)(2,1)S(1)}, bf16[64,384]{1,0:T(8,128)(2,1)S(1)}, u32[]{:S(2)}, u32[]{:S(2)}) collective-permute-start(bf16[64,384]{1,0:T(8,128)(2,1)S(1)} %reshape.325), channel_id=1, source_target_pairs={{32,0},{64,32},{96,64},{128,96},{160,128},{192,160},{224,192},{33,... | collective-permute-start | bytes 147464 | tf_op jit(solution)/shard_map/ppermute | solution.py:11
  165.5 6.1 collective-permute-start.5
  171.6 2.4 copy-start.8
  173.9 479.8 %all-reduce.3.cloned.1.call-start = ((), (), s32[]{:S(2)}) async-start(), calls=%async_computation.3 | async-start | bytes 3538944 | tf_op jit(solution)/shard_map/psum | solution.py:150
  260.6 86.5 %copy-start.13 = (pred[2928]{0:T(1024)(128)(4,1)S(1)}, pred[2928]{0:T(1024)(128)(4,1)}, u32[]{:S(2)}) copy-start(pred[2928]{0:T(1024)(128)(4,1)} %copy-done.12) | copy-start | bytes 8788
  260.7 86.5 %copy-start.15 = (pred[2928]{0:T(1024)(128)(4,1)S(1)}, pred[2928]{0:T(1024)(128)(4,1)}, u32[]{:S(2)}) copy-start(pred[2928]{0:T(1024)(128)(4,1)} %copy-done.14) | copy-start | bytes 8788
  350.6 1.2 copy-start.2
  373.7 6.7 %copy-start.10 = (bf16[64,27,64]{2,0,1:T(8,128)(2,1)S(1)}, bf16[64,27,64]{2,0,1:T(8,128)(2,1)}, u32[]{:S(2)}) copy-start(bf16[64,27,64]{2,0,1:T(8,128)(2,1)} %rev.3) | copy-start | bytes 663556
  373.7 6.6 %copy-start.23 = (u8[6,64,8,8]{1,0,3,2:T(8,128)(4,1)S(1)}, u8[6,64,8,8]{1,0,3,2:T(8,128)(4,1)}, u32[]{:S(2)}) copy-start(u8[6,64,8,8]{1,0,3,2:T(8,128)(4,1)} %get-tuple-element.39) | copy-start | bytes 73732
  380.3 15.2 %copy-start.9 = (bf16[64,27,64]{2,0,1:T(8,128)(2,1)S(1)}, bf16[64,27,64]{2,0,1:T(8,128)(2,1)}, u32[]{:S(2)}) copy-start(bf16[64,27,64]{2,0,1:T(8,128)(2,1)} %param.27) | copy-start | bytes 663556
  406.3 250.7 %copy-start.1 = (bf16[64,27,64]{2,0,1:T(8,128)(2,1)S(1)}, bf16[64,27,64]{2,0,1:T(8,128)(2,1)}, u32[]{:S(2)}) copy-start(bf16[64,27,64]{2,0,1:T(8,128)(2,1)} %param.26) | copy-start | bytes 663556
  653.8 2.3 copy-start.7
Sparse Core Ops, SparseCore 0:
  21.2 88.5 all-gather.3
  161.7 84.9 all-gather.5
  249.8 82.0 all-gather.7
  395.6 258.1 all-reduce.2
where the time goes:
time: 671 us; the launch traced here: 664 us
  waiting for transfers between devices  473 us (70%)
  local copies, waits for them, and re-layouts  102 us (15%)
  matrix products  43 us (6%)
  starting transfers between devices  17.6 us (3%)
  between operations  14.6 us (2%)
  other arithmetic  14 us (2%)
    psum x1, waiting for transfers between devices, residual_block(): lax.psum((first_grad, second_grad), ('group', 'dev'))  246 us
    all_gather x3, waiting for transfers between devices, build_cubes(): piece = lax.all_gather(block, 'dev', axis=1, tiled=True)  226 us
    gather x3, local copies, waits for them, and re-layouts, build_cubes(): picked = jnp.take(piece, jnp.clip(offset_cols, 0, width - 1), axis=1)  43.3 us
    gather x3, local copies, waits for them, and re-layouts, build_cubes(): return jnp.take(cube, jnp.asarray(cube_order), axis=2)  26.5 us
    transpose x2, matrix products, weight_gradient(): jnp.transpose(result, (1, 2, 3, 4, 0)).reshape(outputs, 27 * channels)  21.8 us
    conv_general_dilated x2, matrix products, convolve(): lax.conv_general_dilated(grid, kernel, (1, 1, 1), 'VALID', dimension_numb...  21.2 us
    ppermute x6, starting transfers between devices, from_behind(): lax.ppermute(value, axis, [(source, source + steps) for source in range(f...  17.5 us
  transfers between devices with their start and end apart: 10, of which 5 were waited for; matrix products, arithmetic and copies ran while one was open for 6% of the time, Pallas kernels for 0%

commit v1 on v0

v1 whole, which is shorter than its diff:
```python
import functools

import jax
import jax.numpy as jnp
import numpy as np
from jax import lax
from jax.experimental import pallas as pl
from jax.experimental.pallas import tpu as pltpu
from jax.sharding import PartitionSpec as P

MESH = pl.DeviceIdType.MESH
F32 = jnp.float32
BF16 = jnp.bfloat16
N_Z, N_Y, N_X = 8, 4, 4
PAIRS = 3
DIRECTIONS = [
    (dz, dy, dx)
    for dz in (-1, 0, 1)
    for dy in (-1, 0, 1)
    for dx in (-1, 0, 1)
    if (dz, dy, dx) != (0, 0, 0)
]


def face_of(direction):
    dz, dy, dx = direction
    if dz != 0:
        return (0 if dz == 1 else 1), 2
    if dx != 0:
        return (0 if dx == 1 else 1), 0
    return (0 if dy == 1 else 1), 1


def place():
    d = lax.axis_index("dev")
    return lax.axis_index("group"), d // 8, (d // 2) % 4, d % 2


def device(g, y, x, c):
    return (g, (y * 4 + x) * 2 + c)


def greet(partners):
    barrier = pltpu.get_barrier_semaphore()
    for partner in partners:
        pl.semaphore_signal(barrier, inc=1, device_id=partner, device_id_type=MESH)
    pl.semaphore_wait(barrier, len(partners))


def write_faces(value, scratch, outs, field, fields):
    scratch[...] = value
    cube = value.reshape(8, 8, 8, 128)
    for half, edge in ((0, 0), (1, 7)):
        out = outs[half]
        out[0, 0 * fields + field] = scratch[pl.ds(edge, 64, stride=8), :].astype(BF16)
        out[0, 1 * fields + field] = cube[:, edge].reshape(64, 128).astype(BF16)
        out[0, 2 * fields + field] = value[edge * 64:edge * 64 + 64].astype(BF16)


def live_lanes(count_ref, pair):
    lane = lax.broadcasted_iota(jnp.int32, (1, 128), 1)
    slot = 2 * pair + (lane >= 64).astype(jnp.int32)
    return slot < count_ref[0]


def pack_kernel(count_ref, f_ref, c_ref, x_out, g_out, fa_out, fb_out, scratch):
    pair = pl.program_id(0)
    xt = f_ref[0].astype(F32).T
    x_out[0] = xt.astype(BF16)
    write_faces(xt, scratch, (fa_out, fb_out), 0, 2)
    gt = jnp.where(live_lanes(count_ref, pair), c_ref[0].astype(F32).T, 0.0)
    g_out[0] = gt.astype(BF16)
    write_faces(gt, scratch, (fa_out, fb_out), 1, 2)


def pack(count, features, cotangent):
    blk = lambda *shape: pl.BlockSpec((1,) + shape, lambda p: (p,) + (0,) * len(shape))
    return pl.pallas_call(
        pack_kernel,
        grid=(PAIRS,),
        in_specs=[pl.BlockSpec(memory_space=pltpu.SMEM), blk(128, 512), blk(128, 512)],
        out_specs=[blk(512, 128), blk(512, 128), blk(6, 64, 128), blk(6, 64, 128)],
        out_shape=[
            jax.ShapeDtypeStruct((PAIRS, 512, 128), BF16),
            jax.ShapeDtypeStruct((PAIRS, 512, 128), BF16),
            jax.ShapeDtypeStruct((PAIRS, 6, 64, 128), BF16),
            jax.ShapeDtypeStruct((PAIRS, 6, 64, 128), BF16),
        ],
        scratch_shapes=[pltpu.VMEM((512, 128), F32)],
    )(count, features, cotangent)


def gather_kernel(fields, pos_ref, fa_ref, fb_ref, h_ref, buf_a, buf_b, send, recv):
    g, y, x, c = place()
    bufs, sources = (buf_a, buf_b), (fa_ref, fb_ref)

    def moved(axis, step):
        if axis == "x":
            return device(g, y, (x + step + N_X) % N_X, c)
        return device(g, (y + step + N_Y) % N_Y, x, c)

    below, above = device((g + N_Z - 1) % N_Z, y, x, c), device((g + 1) % N_Z, y, x, c)
    sibling = device(g, y, x, 1 - c)
    greet(
        [below, above, sibling]
        + [moved(axis, step) for axis in ("x", "y") for step in (1, -1)]
    )

    rings = (("x", "y"), ("y", "x"))
    mine = ((x, y), (y, x))

    def block(half, first):
        second = mine[half][1]
        return pl.ds(((c * 4 + second) * 4 + first) * 3, 3)

    def row(half, second):
        return pl.ds((c * 4 + second) * 12, 12)

    started = []

    def copy(half, number, src, dst, target):
        made = pltpu.make_async_remote_copy(
            src_ref=src,
            dst_ref=dst,
            send_sem=send.at[half, number],
            recv_sem=recv.at[half, number],
            device_id=target,
            device_id_type=MESH,
        )
        made.start()
        started.append(made)
        return made

    lower, upper = pl.ds(0, 32), pl.ds(32, 32)
    faces = 3 * fields
    plane = pl.ds(2 * fields, fields)
    sides = pl.ds(0, 2 * fields)
    zs, m = [], [dict(), dict()]
    for half in range(2):
        own = block(half, mine[half][0])
        zs.append(
            copy(
                half,
                0,
                sources[half].at[:, plane],
                bufs[half].at[own, plane],
                below if half == 0 else above,
            )
        )
        bufs[half][own, 0:2 * fields] = sources[half][:, 0:2 * fields]
        bufs[half][96:97] = jnp.zeros((1, faces, 64, 128), BF16)
    for half in range(2):
        own = block(half, mine[half][0])
        zs[half].wait_recv()
        for number, step in ((1, 1), (2, -1)):
            m[half][number] = copy(
                half, number, bufs[half].at[own], bufs[half].at[own],
                moved(rings[half][0], step),
            )
    for number, step, rows in ((3, 1, lower), (4, -1, upper)):
        for half in range(2):
            first = mine[half][0]
            m[half][number - 2].wait_recv()
            came = block(half, (first - step + 4) % 4)
            part = bufs[half].at[came, :, rows]
            m[half][number] = copy(half, number, part, part, moved(rings[half][0], step))
    for half in range(2):
        m[half][3].wait_recv()
        m[half][4].wait_recv()
        line = bufs[half].at[row(half, mine[half][1])]
        for number, step in ((5, 1), (6, -1)):
            m[half][number] = copy(half, number, line, line, moved(rings[half][1], step))
        m[half][9] = copy(half, 9, line, line, sibling)
    for number, step, rows in ((7, 1, lower), (8, -1, upper)):
        for half in range(2):
            second = mine[half][1]
            m[half][number - 2].wait_recv()
            came = row(half, (second - step + 4) % 4)
            part = bufs[half].at[came, :, rows]
            m[half][number] = copy(half, number, part, part, moved(rings[half][1], step))
            line = bufs[half].at[came]
            m[half][number + 3] = copy(half, number + 3, line, line, sibling)
    for number, rows in ((7, lower), (8, upper)):
        for half in range(2):
            m[half][number].wait_recv()
            part = bufs[half].at[row(half, (mine[half][1] + 2) % 4), :, rows]
            m[half][number + 5] = copy(half, number + 5, part, part, sibling)
    for half in range(2):
        for number in range(9, 14):
            m[half][number].wait_recv()
    for made in started:
        made.wait_send()

    def per_slot(slot, carry):
        for k, direction in enumerate(DIRECTIONS):
            half, face = face_of(direction)
            at = pos_ref[slot, k]
            for field in range(fields):
                h_ref[field, slot, k] = bufs[half][at, face * fields + field]
        return carry

    lax.fori_loop(0, 6, per_slot, 0)


def gather(fields, collective_id, pos, fa, fb):
    size = fields * 3 * 64 * 128 * 2 * 97 * 2
    return pl.pallas_call(
        functools.partial(gather_kernel, fields),
        in_specs=[
            pl.BlockSpec(memory_space=pltpu.SMEM),
            pl.BlockSpec(memory_space=pltpu.VMEM),
            pl.BlockSpec(memory_space=pltpu.VMEM),
        ],
        out_specs=pl.BlockSpec(memory_space=pltpu.VMEM),
        out_shape=jax.ShapeDtypeStruct((fields, 6, 26, 64, 128), BF16),
        scratch_shapes=[
            pltpu.VMEM((97, 3 * fields, 64, 128), BF16),
            pltpu.VMEM((97, 3 * fields, 64, 128), BF16),
            pltpu.SemaphoreType.DMA((2, 15)),
            pltpu.SemaphoreType.DMA((2, 15)),
        ],
        compiler_params=pltpu.CompilerParams(
            collective_id=collective_id,
            has_side_effects=True,
            vmem_limit_bytes=size + 16 * 2**20,
        ),
    )(pos, fa, fb)


def build_cube(cube, own, h_ref, par_ref, pair):
    low = lax.broadcasted_iota(jnp.int32, (1, 128), 1) < 64
    cube[1:9, 1:9, 8:16, :] = own.reshape(8, 8, 8, 128)
    for k, (dz, dy, dx) in enumerate(DIRECTIONS):
        if dz != 0 and dy != 0:
            start, count = (0, 16) if dy == 1 else (48, 16)
        else:
            start, count = 0, 64
        picked = []
        for s in range(2):
            value = h_ref[0, s, k, start:start + count].astype(F32)
            turned = pltpu.roll(value, 64, 1)
            picked.append(jnp.where(par_ref[2 * pair + s, k] == s, value, turned))
        piece = jnp.where(low, picked[0], picked[1])
        if count == 16:
            piece = piece[0:8] if dy == 1 else piece[8:16]
        zz = {-1: 0, 1: 9}.get(dz)
        yy = {-1: 0, 1: 9}.get(dy)
        if dx == 0:
            if dz == 0:
                cube[1:9, yy, 8:16, :] = piece.reshape(8, 8, 128)
            elif dy == 0:
                cube[zz, 1:9, 8:16, :] = piece.reshape(8, 8, 128)
            else:
                cube[zz, yy, 8:16, :] = piece
            continue
        sub = 7 if dx == -1 else 16
        edge_x = 7 if dx == -1 else 0
        edge_y = 7 if dy == -1 else 0
        if dz == 0 and dy == 0:
            rows = [(z + 1, q + 1, z * 8 + q) for z in range(8) for q in range(8)]
        elif dz == 0:
            rows = [(z + 1, yy, z * 8 + edge_y) for z in range(8)]
        elif dy == 0:
            rows = [(zz, q + 1, q * 8 + edge_x) for q in range(8)]
        else:
            rows = [(zz, yy, edge_x)]
        for a, b, r in rows:
            cube[a, b, sub:sub + 1, :] = piece[r:r + 1]


def stack_taps(cube, taps):
    for ty in range(3):
        for tx in range(3):
            part = cube[:, ty:ty + 8, 7 + tx:15 + tx, :].reshape(640, 128)
            column = (ty * 3 + tx) * 128
            taps[:, column:column + 128] = part.astype(BF16)


def convolve(taps, w_ref):
    wide = jnp.dot(taps[...], w_ref[...], preferred_element_type=F32)
    return wide[0:512, 0:128] + wide[64:576, 128:256] + wide[128:640, 256:384]


def spread(wide_g, value):
    for tz in range(3):
        wide_g[tz * 64:tz * 64 + 512, tz * 128:tz * 128 + 128] = value


def clear_spread(wide_g):
    wide_g[...] = jnp.zeros((640, 384), BF16)


def outer(wide_g, taps):
    return lax.dot_general(
        wide_g[...], taps[...], (((0,), (0,)), ((), ())), preferred_element_type=F32
    )


def first_kernel(count_ref, par_ref, x_ref, g_ref, hx_ref, hg_ref, w_ref, v_ref,
                 h_out, fa_out, fb_out, m_out, cube, taps, taps_g, wide_g, scratch):
    pair = pl.program_id(0)
    build_cube(cube, x_ref[0].astype(F32), hx_ref, par_ref, pair)
    stack_taps(cube, taps)
    first = convolve(taps, w_ref)
    hidden = jnp.where(live_lanes(count_ref, pair), jnp.maximum(first, 0.0), 0.0)
    hidden = hidden.astype(BF16).astype(F32)
    h_out[0] = hidden.astype(BF16)
    write_faces(hidden, scratch, (fa_out, fb_out), 0, 1)
    build_cube(cube, g_ref[0].astype(F32), hg_ref, par_ref, pair)
    stack_taps(cube, taps_g)
    back = convolve(taps_g, v_ref)
    hidden_grad = jnp.where(scratch[...] > 0, back, 0.0).astype(BF16)

    @pl.when(pair == 0)
    def _():
        clear_spread(wide_g)
        m_out[...] = jnp.zeros_like(m_out)

    spread(wide_g, hidden_grad)
    m_out[...] += outer(wide_g, taps)


def blocked(*shape):
    return pl.BlockSpec((1,) + shape, lambda p: (p,) + (0,) * len(shape))


def fixed(*shape):
    return pl.BlockSpec(shape, lambda p: (0,) * len(shape))


def halo_spec(field):
    return pl.BlockSpec((1, 2, 26, 64, 128), lambda p: (field, p, 0, 0, 0))


def first_part(count, parity, xt, gt, halos, w, v):
    smem = pl.BlockSpec(memory_space=pltpu.SMEM)
    return pl.pallas_call(
        first_kernel,
        grid=(PAIRS,),
        in_specs=[smem, smem, blocked(512, 128), blocked(512, 128), halo_spec(0),
                  halo_spec(1), fixed(1152, 384), fixed(1152, 384)],
        out_specs=[blocked(512, 128), blocked(3, 64, 128), blocked(3, 64, 128),
                   fixed(384, 1152)],
        out_shape=[
            jax.ShapeDtypeStruct((PAIRS, 512, 128), BF16),
            jax.ShapeDtypeStruct((PAIRS, 3, 64, 128), BF16),
            jax.ShapeDtypeStruct((PAIRS, 3, 64, 128), BF16),
            jax.ShapeDtypeStruct((384, 1152), F32),
        ],
        scratch_shapes=[
            pltpu.VMEM((10, 10, 24, 128), F32),
            pltpu.VMEM((640, 1152), BF16),
            pltpu.VMEM((640, 1152), BF16),
            pltpu.VMEM((640, 384), BF16),
            pltpu.VMEM((512, 128), F32),
        ],
        compiler_params=pltpu.CompilerParams(vmem_limit_bytes=40 * 2**20),
    )(count, parity, xt, gt, halos, halos, w, v)


def second_kernel(count_ref, par_ref, f_ref, h_ref, g_ref, hh_ref, w_ref, m1_ref,
                  o_out, p_out, cube, taps, wide_g, total):
    pair = pl.program_id(0)
    build_cube(cube, h_ref[0].astype(F32), hh_ref, par_ref, pair)
    stack_taps(cube, taps)
    second = convolve(taps, w_ref)
    slot = 2 * pair + (lax.broadcasted_iota(jnp.int32, (128, 1), 0) >= 64).astype(jnp.int32)
    result = f_ref[0].astype(F32) + second.T
    o_out[0] = jnp.where(slot < count_ref[0], result, 0.0).astype(BF16)

    @pl.when(pair == 0)
    def _():
        clear_spread(wide_g)
        total[...] = jnp.zeros_like(total)

    spread(wide_g, g_ref[0])
    total[...] += outer(wide_g, taps)

    @pl.when(pair == PAIRS - 1)
    def _():
        low = lax.broadcasted_iota(jnp.int32, (1, 128), 1) < 64
        for q in range(9):
            for tz in range(3):
                even, odd = pl.ds(tz * 128, 64), pl.ds(tz * 128 + 64, 64)
                lanes = pl.ds(q * 128, 128)
                one = m1_ref[even, lanes] + pltpu.roll(m1_ref[odd, lanes], 64, 1)
                two = pltpu.roll(total[even, lanes], 64, 1) + total[odd, lanes]
                p_out[pl.ds((q * 3 + tz) * 64, 64), :] = jnp.where(low, one, two)
        p_out[1728:2048, :] = jnp.zeros((320, 128), F32)


def second_part(count, parity, features, ht, gt, halos, v, m1):
    smem = pl.BlockSpec(memory_space=pltpu.SMEM)
    return pl.pallas_call(
        second_kernel,
        grid=(PAIRS,),
        in_specs=[smem, smem, blocked(128, 512), blocked(512, 128), blocked(512, 128),
                  halo_spec(0), fixed(1152, 384), fixed(384, 1152)],
        out_specs=[blocked(128, 512), fixed(2048, 128)],
        out_shape=[
            jax.ShapeDtypeStruct((PAIRS, 128, 512), BF16),
            jax.ShapeDtypeStruct((2048, 128), F32),
        ],
        scratch_shapes=[
            pltpu.VMEM((10, 10, 24, 128), F32),
            pltpu.VMEM((640, 1152), BF16),
            pltpu.VMEM((640, 384), BF16),
            pltpu.VMEM((384, 1152), F32),
        ],
        compiler_params=pltpu.CompilerParams(vmem_limit_bytes=40 * 2**20),
    )(count, parity, features, ht, gt, halos, v, m1)


def reduce_kernel(p_ref, out_ref, r1, a1, r2, a2, r3, r4, whole, send, recv):
    g, y, x, c = place()
    sibling = device(g, y, x, 1 - c)
    xs = [device(g, y, (x + k) % N_X, c) for k in range(1, N_X)]
    ys = [device(g, (y + k) % N_Y, x, c) for k in range(1, N_Y)]
    zs = [device((g + k) % N_Z, y, x, c) for k in range(1, N_Z)]
    greet([sibling] + xs + ys + zs)
    used = [0]

    def copy(src, dst, target):
        number = used[0]
        used[0] += 1
        made = pltpu.make_async_remote_copy(
            src_ref=src, dst_ref=dst, send_sem=send.at[number], recv_sem=recv.at[number],
            device_id=target, device_id_type=MESH,
        )
        made.start()
        return made

    copy(p_ref.at[pl.ds((1 - c) * 1024, 1024)], r1, sibling).wait()
    a1[...] = (p_ref[pl.ds(c * 1024, 1024)] + r1[...]).astype(BF16)

    made = [
        copy(a1.at[pl.ds(((x + k) % N_X) * 256, 256)], r2.at[k - 1], xs[k - 1])
        for k in range(1, N_X)
    ]
    for one in made:
        one.wait()
    part = a1[pl.ds(x * 256, 256)].astype(F32)
    for k in range(3):
        part = part + r2[k].astype(F32)
    a2[...] = part

    made = [
        copy(a2.at[pl.ds(((y + k) % N_Y) * 64, 64)], r3.at[k - 1], ys[k - 1])
        for k in range(1, N_Y)
    ]
    for one in made:
        one.wait()
    part = a2[pl.ds(y * 64, 64)]
    for k in range(3):
        part = part + r3[k]
    r4[g] = part.astype(BF16)

    made = [copy(r4.at[g], r4.at[g], zs[k - 1]) for k in range(1, N_Z)]
    for one in made:
        one.wait()
    part = r4[0].astype(F32)
    for k in range(1, N_Z):
        part = part + r4[k].astype(F32)
    start = ((c * 4 + x) * 4 + y) * 64
    whole[pl.ds(start, 64)] = part.astype(BF16)

    for rows, targets in (
        (pl.ds(start, 64), ys),
        (pl.ds((c * 4 + x) * 256, 256), xs),
        (pl.ds(c * 1024, 1024), [sibling]),
    ):
        made = [copy(whole.at[rows], whole.at[rows], target) for target in targets]
        for one in made:
            one.wait()
    out_ref[...] = whole[...]


def reduce_all(p):
    return pl.pallas_call(
        reduce_kernel,
        in_specs=[pl.BlockSpec(memory_space=pltpu.VMEM)],
        out_specs=pl.BlockSpec(memory_space=pltpu.VMEM),
        out_shape=jax.ShapeDtypeStruct((2048, 128), BF16),
        scratch_shapes=[
            pltpu.VMEM((1024, 128), F32),
            pltpu.VMEM((1024, 128), BF16),
            pltpu.VMEM((3, 256, 128), BF16),
            pltpu.VMEM((256, 128), F32),
            pltpu.VMEM((3, 64, 128), F32),
            pltpu.VMEM((N_Z, 64, 128), BF16),
            pltpu.VMEM((2048, 128), BF16),
            pltpu.SemaphoreType.DMA((24,)),
            pltpu.SemaphoreType.DMA((24,)),
        ],
        compiler_params=pltpu.CompilerParams(
            collective_id=2, has_side_effects=True, vmem_limit_bytes=16 * 2**20
        ),
    )(p)


def block_weight(w):
    turned = jnp.transpose(w, (2, 3, 4, 1, 0))[:, :, None, :, :, None, :]
    same = jnp.eye(2, dtype=w.dtype)[None, None, :, None, None, :, None]
    return (turned * same).reshape(1152, 384)


def halo_places(neighbours):
    halves = jnp.asarray(np.array([face_of(d)[0] for d in DIRECTIONS], np.int32))[None, :]
    dev = neighbours // 6 % 32
    y, x, c = dev // 8, dev // 2 % 4, dev % 2
    first = jnp.where(halves == 0, x, y)
    second = jnp.where(halves == 0, y, x)
    pos = ((c * 4 + second) * 4 + first) * 3 + neighbours % 6 // 2
    return jnp.where(neighbours >= 0, pos, 96).astype(jnp.int32), neighbours % 2


def per_device(features, cotangent, first_weight, second_weight, counts, neighbours):
    count = counts[lax.axis_index("group"), lax.axis_index("dev")].reshape(1)
    pos, parity = halo_places(neighbours)
    w1 = first_weight.reshape(64, 3, 3, 3, 64)
    w2 = second_weight.reshape(64, 3, 3, 3, 64)
    wide1, wide2 = block_weight(w1), block_weight(w2)
    wide_back = block_weight(jnp.transpose(w2[:, ::-1, ::-1, ::-1, :], (4, 1, 2, 3, 0)))
    feats = features.reshape(PAIRS, 128, 512)
    xt, gt, fa, fb = pack(count, feats, cotangent.reshape(PAIRS, 128, 512))
    halos = gather(2, 0, pos, fa, fb)
    ht, ha, hb, m1 = first_part(count, parity, xt, gt, halos, wide1, wide_back)
    halos_h = gather(1, 1, pos, ha, hb)
    out, p = second_part(count, parity, feats, ht, gt, halos_h, wide2, m1)
    total = reduce_all(p)
    total = total[:1728].reshape(3, 3, 3, 64, 2, 64)
    grads = jnp.transpose(total, (4, 3, 2, 0, 1, 5)).reshape(2, 64, 27, 64).astype(F32)
    return out.reshape(6, 64, 512), grads[0], grads[1]


def solution(mesh):
    placed = (
        P(("group", "dev"), None, None),
        P(("group", "dev"), None, None),
        P(),
        P(),
        P(),
        P(("group", "dev"), None),
    )
    return jax.shard_map(
        per_device,
        mesh=mesh,
        in_specs=placed,
        out_specs=(P(("group", "dev"), None, None), P(), P()),
        check_vma=False,
    )
```

time: 671 us -> 190 us (0.28); the launches traced: 664 us -> 189 us
  waiting for transfers between devices: 473 us -> 0 us
  Pallas kernels: 0 us -> 163 us
  local copies, waits for them, and re-layouts: 102 us -> 18.3 us
  matrix products: 43 us -> 0 us
  starting transfers between devices: 17.6 us -> 0 us
  between operations: 14.6 us -> 0.85 us
    psum x1 -> x0, waiting for transfers between devices: 246 us -> none  [residual_block(): lax.psum((first_grad, second_grad), ('group', 'dev'))]
    all_gather x3 -> x0, waiting for transfers between devices: 226 us -> none  [build_cubes(): piece = lax.all_gather(block, 'dev', axis=1, tiled=True)]
    pallas_call x0 -> x6, Pallas kernels: none -> 163 us  [the longest x2 107 us: gather(): pl.pallas_call(functools.partial(gather_kernel, fields), in_specs=[pl.Blo...]
    gather x11 -> x0, local copies, waits for them, and re-layouts: 77.1 us -> none  [the longest x3 43.3 us: build_cubes(): picked = jnp.take(piece, jnp.clip(offset_cols, 0, width - 1), axis=1)]
    transpose x2 -> x0, matrix products: 21.8 us -> none  [weight_gradient(): jnp.transpose(result, (1, 2, 3, 4, 0)).reshape(outputs, 27 * channels)]
    conv_general_dilated x2 -> x0, matrix products: 21.2 us -> none  [convolve(): lax.conv_general_dilated(grid, kernel, (1, 1, 1), 'VALID', dimension_numb...]
    ppermute x6 -> x0, starting transfers between devices: 17.5 us -> none  [from_behind(): lax.ppermute(value, axis, [(source, source + steps) for source in range(f...]
    unnamed x54 -> x14, local copies, waits for them, and re-layouts: 9.03 us -> 0.04 us
  transfers between devices with their start and end apart: 10 -> 0, of which waited for: 5 -> 0; matrix products, arithmetic and copies ran while one was open for 6% -> 0% of each run, Pallas kernels for 0% -> 0%
where the time goes in v1:
time: 190 us; the launch traced here: 189 us
  Pallas kernels  163 us (86%)
  local copies, waits for them, and re-layouts  18.3 us (10%)
  other arithmetic  7.43 us (4%)
    pallas_call x2, Pallas kernels, gather(): pl.pallas_call(functools.partial(gather_kernel, fields), in_specs=[pl.Blo...  107 us
    pallas_call x1, Pallas kernels, reduce_all(): pl.pallas_call(reduce_kernel, in_specs=[pl.BlockSpec(memory_space=pltpu.V...  31.5 us
    pallas_call x1, Pallas kernels, first_part(): pl.pallas_call(first_kernel, grid=(PAIRS,), in_specs=[smem, smem, blocked...  10.9 us
    pallas_call x1, Pallas kernels, second_part(): pl.pallas_call(second_kernel, grid=(PAIRS,), in_specs=[smem, smem, blocke...  9.35 us
    mul x3, local copies, waits for them, and re-layouts, block_weight(): return (turned * same).reshape(1152, 384)  8.35 us
    mul x1, other arithmetic, block_weight(): return (turned * same).reshape(1152, 384)  6.64 us
    slice x3, local copies, waits for them, and re-layouts, per_device(): return (out.reshape(6, 64, 512), grads[0], grads[1])  3.96 us
    pallas_call x1, Pallas kernels, pack(): pl.pallas_call(pack_kernel, grid=(PAIRS,), in_specs=[pl.BlockSpec(memory_...  3.89 us

profile of v1, /device:TPU:1, one launch (start us, length us, event | category | flops | bytes accessed | tf_op | source)
XLA Modules:
  0.0 189.4 jit_solution(7901886224180528945)
XLA Ops:
  0.6 0.0 copy-start.5
  0.6 0.0 copy-start.6
  0.7 1.4 dynamic_slice.3
  2.0 0.7 fusion.8
  2.8 1.0 reverse_bitcast_fusion
  3.8 0.4 copy.11
  4.2 0.0 copy-done.6
  4.2 0.9 copy.10
  5.1 0.0 copy-done.5
  5.1 1.3 copy.12
  6.4 3.9 %shard_map.94 = (bf16[3,512,128]{2,1,0:T(8,128)(2,1)}, bf16[3,512,128]{2,1,0:T(8,128)(2,1)}, bf16[3,6,64,128]{3,2,1,0:T(8,128)(2,1)}, bf16[3,6,64,128]{3,2,1,0:T(8,128)(2,1)}) custom-call(s32[1]{0:T(128)} %bitcast.count_ref, bf16[3,128,512]{2,1,0:T(8,128)(2,1)} %bitcast.15, bf16[3,128,512]{2,1,0:T(8,128)(2,1)} %bitcast.23), custom_call_target="tpu_custom_call" | custom-call | tf_op jit(solution)/shard_map/pallas_call | solution.py:78
  10.3 6.6 %broadcast_multiply_fusion = (bf16[3,3,2,64,3,2,64]{6,5,4,3,2,1,0:T(2,128)(2,1)}, bf16[3,3,2,64,3,2,64]{6,5,4,3,2,1,0:T(2,128)(2,1)S(1)}, bf16[3,3,2,64,3,2,64]{6,5,4,3,2,1,0:T(2,128)(2,1)}) fusion(bf16[3,3,64,3,64]{4,3,2,1,0:T(4,128)(2,1)} %copy.12, bf16[2,2]{1,0:T(2,128)(2,1)S(1)} %compare_convert_fusion, bf16[3,3,64,3,64]{4,3,2,1,0:T(4,128)(2,1)S(1)} %copy.11, ...), kind=kLoop, calls=%fused_computation | loop fusion | flops 1327104 | bytes 3317768 | tf_op jit(solution)/shard_map/mul | solution.py:504
  16.9 3.6 %mul.73.w_ref = bf16[1152,384]{1,0:T(8,128)(2,1)S(1)} reshape(bf16[3,3,2,64,3,2,64]{6,5,4,3,2,1,0:T(2,128)(2,1)} %get-tuple-element.27) | data formatting | bytes 1769472 | tf_op jit(solution)/shard_map/mul | solution.py:504
  20.5 1.1 mul.70.v_ref
  21.6 0.0 copy-start.3
  21.6 0.0 copy-start.4
  21.7 3.7 %mul.67.w_ref = bf16[1152,384]{1,0:T(8,128)(2,1)S(1)} reshape(bf16[3,3,2,64,3,2,64]{6,5,4,3,2,1,0:T(2,128)(2,1)} %get-tuple-element.29) | data formatting | bytes 1769472 | tf_op jit(solution)/shard_map/mul | solution.py:504
  25.3 0.0 copy-done.3
  25.3 0.0 copy-done.4
  25.3 0.0 copy-start
  25.4 0.0 copy-start.2
  25.4 69.1 %shard_map.95.hx_ref.hg_ref = bf16[2,6,26,64,128]{4,3,2,1,0:T(8,128)(2,1)S(1)} custom-call(s32[6,26]{1,0:T(8,128)S(1)} %get-tuple-element.25.pos_ref, bf16[3,6,64,128]{3,2,1,0:T(8,128)(2,1)S(1)} %copy-done.3, bf16[3,6,64,128]{3,2,1,0:T(8,128)(2,1)S(1)} %copy-done.4), custom_call_target="tpu_custom_call" | custom-call | tf_op jit(solution)/shard_map/pallas_call | solution.py:207
  94.5 0.0 copy-done
  94.5 0.0 copy-done.2
  94.5 10.9 %shard_map.96 = (bf16[3,512,128]{2,1,0:T(8,128)(2,1)S(1)}, bf16[3,3,64,128]{3,2,1,0:T(8,128)(2,1)S(1)}, bf16[3,3,64,128]{3,2,1,0:T(8,128)(2,1)S(1)}, f32[384,1152]{1,0:T(8,128)S(1)}) custom-call(s32[1]{0:T(128)} %bitcast.count_ref, s32[6,26]{1,0:T(8,128)S(1)} %get-tuple-element.26.par_ref, bf16[3,512,128]{2,1,0:T(8,128)(2,1)S(1)} %copy-done.2, ...), custom_call_target="tpu_custom_call" | custom-call | tf_op jit(solution)/shard_map/pallas_call | solution.py:337
  105.5 0.0 copy-start.1
  105.5 38.0 %shard_map.97.hh_ref = bf16[1,6,26,64,128]{4,3,2,1,0:T(8,128)(2,1)S(1)} custom-call(s32[6,26]{1,0:T(8,128)S(1)} %get-tuple-element.25.pos_ref, bf16[3,3,64,128]{3,2,1,0:T(8,128)(2,1)S(1)} %get-tuple-element.18.fa_ref, bf16[3,3,64,128]{3,2,1,0:T(8,128)(2,1)S(1)} %get-tuple-element.19.fb_ref), custom_call_target="tpu_custom_call" | custom-call | tf_op jit(solution)/shard_map/pallas_call | solution.py:207
  143.5 0.0 copy-done.1
  143.5 9.3 %shard_map.98 = (bf16[3,128,512]{2,1,0:T(8,128)(2,1)}, f32[2048,128]{1,0:T(8,128)S(1)}) custom-call(s32[1]{0:T(128)} %bitcast.count_ref, s32[6,26]{1,0:T(8,128)S(1)} %get-tuple-element.26.par_ref, bf16[3,128,512]{2,1,0:T(8,128)(2,1)S(1)} %bitcast.16, bf16[3,512,128]{2,1,0:T(8,128)(2,1)S(1)} %get-tuple-element.17.h_ref, bf16[3,512,128]{2,1,0:T(8,128)(2,1)S(1)} %copy-done, ...), custom_call_target="tpu_custom_call" | custom-call | tf_op jit(solution)/shard_map/pallas_call | solution.py:394
  152.9 31.5 %shard_map.99 = bf16[2048,128]{1,0:T(8,128)(2,1)S(1)} custom-call(f32[2048,128]{1,0:T(8,128)S(1)} %get-tuple-element.22.p_ref), custom_call_target="tpu_custom_call" | custom-call | tf_op jit(solution)/shard_map/pallas_call | solution.py:479
  184.4 0.1 slice_convert_fusion
  184.4 1.0 reshape.60
  185.4 1.9 %fusion.18 = (f32[1,64,3,3,3,64]{5,0,1,2,4,3:T(1,128)S(1)}, f32[1,64,3,3,3,64]{5,0,1,2,4,3:T(1,128)S(1)}) fusion(f32[2,64,3,3,3,64]{5,0,1,2,4,3:T(2,128)S(1)} %bitcast.17), kind=kLoop, calls=%fused_computation.50 | loop fusion | bytes 1769472 | tf_op jit(solution)/shard_map/slice | solution.py:533
  187.4 1.0 copy.14
  188.4 1.0 copy.13
  (1 shorter events, 0.0 us)
Async XLA Ops:
  0.6 4.5 %copy-start.5 = (bf16[64,27,64]{2,0,1:T(8,128)(2,1)S(1)}, bf16[64,27,64]{2,0,1:T(8,128)(2,1)}, u32[]{:S(2)}) copy-start(bf16[64,27,64]{2,0,1:T(8,128)(2,1)} %param.10) | copy-start | bytes 663556
  0.6 3.5 %copy-start.6 = (bf16[64,27,64]{2,0,1:T(8,128)(2,1)S(1)}, bf16[64,27,64]{2,0,1:T(8,128)(2,1)}, u32[]{:S(2)}) copy-start(bf16[64,27,64]{2,0,1:T(8,128)(2,1)} %param.9) | copy-start | bytes 663556
  21.6 3.7 %copy-start.3 = (bf16[3,6,64,128]{3,2,1,0:T(8,128)(2,1)S(1)}, bf16[3,6,64,128]{3,2,1,0:T(8,128)(2,1)}, u32[]{:S(2)}) copy-start(bf16[3,6,64,128]{3,2,1,0:T(8,128)(2,1)} %get-tuple-element.15.fa_ref) | copy-start | bytes 884740
  21.6 3.7 %copy-start.4 = (bf16[3,6,64,128]{3,2,1,0:T(8,128)(2,1)S(1)}, bf16[3,6,64,128]{3,2,1,0:T(8,128)(2,1)}, u32[]{:S(2)}) copy-start(bf16[3,6,64,128]{3,2,1,0:T(8,128)(2,1)} %get-tuple-element.16.fb_ref) | copy-start | bytes 884740
  25.3 69.2 %copy-start = (bf16[3,512,128]{2,1,0:T(8,128)(2,1)S(1)}, bf16[3,512,128]{2,1,0:T(8,128)(2,1)}, u32[]{:S(2)}) copy-start(bf16[3,512,128]{2,1,0:T(8,128)(2,1)} %get-tuple-element.14.g_ref) | copy-start | bytes 1179652
  25.4 69.2 %copy-start.2 = (bf16[3,512,128]{2,1,0:T(8,128)(2,1)S(1)}, bf16[3,512,128]{2,1,0:T(8,128)(2,1)}, u32[]{:S(2)}) copy-start(bf16[3,512,128]{2,1,0:T(8,128)(2,1)} %get-tuple-element.13.x_ref) | copy-start | bytes 1179652
  105.5 38.1 %copy-start.1 = (bf16[6,64,512]{2,1,0:T(8,128)(2,1)S(1)}, bf16[6,64,512]{2,1,0:T(8,128)(2,1)}, u32[]{:S(2)}) copy-start(bf16[6,64,512]{2,1,0:T(8,128)(2,1)} %param.7) | copy-start | bytes 1179652

commit v2 on v1

--- a/solution.py
+++ b/solution.py
@@ -57,10 +57,14 @@
         out[0, 2 * fields + field] = value[edge * 64:edge * 64 + 64].astype(BF16)
 
 
+def own_count(count_ref):
+    return count_ref[lax.axis_index("group"), lax.axis_index("dev")]
+
+
 def live_lanes(count_ref, pair):
     lane = lax.broadcasted_iota(jnp.int32, (1, 128), 1)
     slot = 2 * pair + (lane >= 64).astype(jnp.int32)
-    return slot < count_ref[0]
+    return slot < own_count(count_ref)
 
 
 def pack_kernel(count_ref, f_ref, c_ref, x_out, g_out, fa_out, fb_out, scratch):
@@ -276,8 +280,26 @@
             taps[:, column:column + 128] = part.astype(BF16)
 
 
-def convolve(taps, w_ref):
-    wide = jnp.dot(taps[...], w_ref[...], preferred_element_type=F32)
+def tap_of(w_ref, tap):
+    value = w_ref[tap].astype(F32)
+    return jnp.concatenate([value, value], axis=1)
+
+
+def widen(w_ref, wide, backward):
+    low = lax.broadcasted_iota(jnp.int32, (1, 128), 1) < 64
+    for tz in range(3):
+        for q in range(9):
+            tap = tz * 9 + q
+            value = tap_of(w_ref, 26 - tap if backward else tap)
+            a, b = (q, tz) if backward else (tz, q)
+            lanes = pl.ds(b * 128, 128)
+            wide[pl.ds(a * 128, 64), lanes] = jnp.where(low, value, 0.0).astype(BF16)
+            wide[pl.ds(a * 128 + 64, 64), lanes] = jnp.where(low, 0.0, value).astype(BF16)
+
+
+def convolve(taps, wide, backward=False):
+    contract = (((1,), (0 if backward else 1,)), ((), ()))
+    wide = lax.dot_general(taps[...], wide[...], contract, preferred_element_type=F32)
     return wide[0:512, 0:128] + wide[64:576, 128:256] + wide[128:640, 256:384]
 
 
@@ -297,18 +319,24 @@
 
 
 def first_kernel(count_ref, par_ref, x_ref, g_ref, hx_ref, hg_ref, w_ref, v_ref,
-                 h_out, fa_out, fb_out, m_out, cube, taps, taps_g, wide_g, scratch):
+                 h_out, fa_out, fb_out, m_out, cube, taps, taps_g, wide_g, scratch, wide_w, wide_v):
     pair = pl.program_id(0)
+
+    @pl.when(pair == 0)
+    def _():
+        widen(w_ref, wide_w, False)
+        widen(v_ref, wide_v, True)
+
     build_cube(cube, x_ref[0].astype(F32), hx_ref, par_ref, pair)
     stack_taps(cube, taps)
-    first = convolve(taps, w_ref)
+    first = convolve(taps, wide_w)
     hidden = jnp.where(live_lanes(count_ref, pair), jnp.maximum(first, 0.0), 0.0)
     hidden = hidden.astype(BF16).astype(F32)
     h_out[0] = hidden.astype(BF16)
     write_faces(hidden, scratch, (fa_out, fb_out), 0, 1)
     build_cube(cube, g_ref[0].astype(F32), hg_ref, par_ref, pair)
     stack_taps(cube, taps_g)
-    back = convolve(taps_g, v_ref)
+    back = convolve(taps_g, wide_v, True)
     hidden_grad = jnp.where(scratch[...] > 0, back, 0.0).astype(BF16)
 
     @pl.when(pair == 0)
@@ -332,13 +360,13 @@
     return pl.BlockSpec((1, 2, 26, 64, 128), lambda p: (field, p, 0, 0, 0))
 
 
-def first_part(count, parity, xt, gt, halos, w, v):
+def first_part(counts, parity, xt, gt, halos, w, v):
     smem = pl.BlockSpec(memory_space=pltpu.SMEM)
     return pl.pallas_call(
         first_kernel,
         grid=(PAIRS,),
         in_specs=[smem, smem, blocked(512, 128), blocked(512, 128), halo_spec(0),
-                  halo_spec(1), fixed(1152, 384), fixed(1152, 384)],
+                  halo_spec(1), fixed(27, 64, 64), fixed(27, 64, 64)],
         out_specs=[blocked(512, 128), blocked(3, 64, 128), blocked(3, 64, 128),
                    fixed(384, 1152)],
         out_shape=[
@@ -353,20 +381,27 @@
             pltpu.VMEM((640, 1152), BF16),
             pltpu.VMEM((640, 384), BF16),
             pltpu.VMEM((512, 128), F32),
+            pltpu.VMEM((384, 1152), BF16),
+            pltpu.VMEM((1152, 384), BF16),
         ],
         compiler_params=pltpu.CompilerParams(vmem_limit_bytes=40 * 2**20),
-    )(count, parity, xt, gt, halos, halos, w, v)
+    )(counts, parity, xt, gt, halos, halos, w, v)
 
 
 def second_kernel(count_ref, par_ref, f_ref, h_ref, g_ref, hh_ref, w_ref, m1_ref,
-                  o_out, p_out, cube, taps, wide_g, total):
+                  o_out, p_out, cube, taps, wide_g, total, wide_w):
     pair = pl.program_id(0)
+
+    @pl.when(pair == 0)
+    def _():
+        widen(w_ref, wide_w, False)
+
     build_cube(cube, h_ref[0].astype(F32), hh_ref, par_ref, pair)
     stack_taps(cube, taps)
-    second = convolve(taps, w_ref)
+    second = convolve(taps, wide_w)
     slot = 2 * pair + (lax.broadcasted_iota(jnp.int32, (128, 1), 0) >= 64).astype(jnp.int32)
     result = f_ref[0].astype(F32) + second.T
-    o_out[0] = jnp.where(slot < count_ref[0], result, 0.0).astype(BF16)
+    o_out[0] = jnp.where(slot < own_count(count_ref), result, 0.0).astype(BF16)
 
     @pl.when(pair == 0)
     def _():
@@ -389,13 +424,13 @@
         p_out[1728:2048, :] = jnp.zeros((320, 128), F32)
 
 
-def second_part(count, parity, features, ht, gt, halos, v, m1):
+def second_part(counts, parity, features, ht, gt, halos, v, m1):
     smem = pl.BlockSpec(memory_space=pltpu.SMEM)
     return pl.pallas_call(
         second_kernel,
         grid=(PAIRS,),
         in_specs=[smem, smem, blocked(128, 512), blocked(512, 128), blocked(512, 128),
-                  halo_spec(0), fixed(1152, 384), fixed(384, 1152)],
+                  halo_spec(0), fixed(27, 64, 64), fixed(384, 1152)],
         out_specs=[blocked(128, 512), fixed(2048, 128)],
         out_shape=[
             jax.ShapeDtypeStruct((PAIRS, 128, 512), BF16),
@@ -406,18 +441,23 @@
             pltpu.VMEM((640, 1152), BF16),
             pltpu.VMEM((640, 384), BF16),
             pltpu.VMEM((384, 1152), F32),
+            pltpu.VMEM((384, 1152), BF16),
         ],
         compiler_params=pltpu.CompilerParams(vmem_limit_bytes=40 * 2**20),
-    )(count, parity, features, ht, gt, halos, v, m1)
-
-
-def reduce_kernel(p_ref, out_ref, r1, a1, r2, a2, r3, r4, whole, send, recv):
+    )(counts, parity, features, ht, gt, halos, v, m1)
+
+
+def reduce_kernel(p_ref, first_out, second_out, r1, a1, r2, r4, whole, send, recv):
     g, y, x, c = place()
     sibling = device(g, y, x, 1 - c)
-    xs = [device(g, y, (x + k) % N_X, c) for k in range(1, N_X)]
-    ys = [device(g, (y + k) % N_Y, x, c) for k in range(1, N_Y)]
+    layer = [
+        ((y + ky) % N_Y, (x + kx) % N_X, ky * N_X + kx)
+        for ky in range(N_Y)
+        for kx in range(N_X)
+        if (ky, kx) != (0, 0)
+    ]
     zs = [device((g + k) % N_Z, y, x, c) for k in range(1, N_Z)]
-    greet([sibling] + xs + ys + zs)
+    greet([sibling] + [device(g, yy, xx, c) for yy, xx, _ in layer] + zs)
     used = [0]
 
     def copy(src, dst, target):
@@ -434,74 +474,59 @@
     a1[...] = (p_ref[pl.ds(c * 1024, 1024)] + r1[...]).astype(BF16)
 
     made = [
-        copy(a1.at[pl.ds(((x + k) % N_X) * 256, 256)], r2.at[k - 1], xs[k - 1])
-        for k in range(1, N_X)
+        copy(a1.at[pl.ds((yy * N_X + xx) * 64, 64)], r2.at[k], device(g, yy, xx, c))
+        for yy, xx, k in layer
     ]
     for one in made:
         one.wait()
-    part = a1[pl.ds(x * 256, 256)].astype(F32)
-    for k in range(3):
+    at = y * N_X + x
+    part = a1[pl.ds(at * 64, 64)].astype(F32)
+    for k in range(1, 16):
         part = part + r2[k].astype(F32)
-    a2[...] = part
-
-    made = [
-        copy(a2.at[pl.ds(((y + k) % N_Y) * 64, 64)], r3.at[k - 1], ys[k - 1])
-        for k in range(1, N_Y)
-    ]
-    for one in made:
-        one.wait()
-    part = a2[pl.ds(y * 64, 64)]
-    for k in range(3):
-        part = part + r3[k]
     r4[g] = part.astype(BF16)
 
-    made = [copy(r4.at[g], r4.at[g], zs[k - 1]) for k in range(1, N_Z)]
+    made = [copy(r4.at[g], r4.at[g], target) for target in zs]
     for one in made:
         one.wait()
     part = r4[0].astype(F32)
     for k in range(1, N_Z):
         part = part + r4[k].astype(F32)
-    start = ((c * 4 + x) * 4 + y) * 64
-    whole[pl.ds(start, 64)] = part.astype(BF16)
-
-    for rows, targets in (
-        (pl.ds(start, 64), ys),
-        (pl.ds((c * 4 + x) * 256, 256), xs),
-        (pl.ds(c * 1024, 1024), [sibling]),
-    ):
-        made = [copy(whole.at[rows], whole.at[rows], target) for target in targets]
-        for one in made:
-            one.wait()
-    out_ref[...] = whole[...]
+    rows = pl.ds(c * 1024 + at * 64, 64)
+    whole[rows] = part.astype(BF16)
+
+    made = [
+        copy(whole.at[rows], whole.at[rows], device(g, yy, xx, c)) for yy, xx, _ in layer
+    ]
+    for one in made:
+        one.wait()
+    half = pl.ds(c * 1024, 1024)
+    copy(whole.at[half], whole.at[half], sibling).wait()
+    for q in range(9):
+        for tz in range(3):
+            value = whole[pl.ds((q * 3 + tz) * 64, 64)].astype(F32)
+            first_out[tz * 9 + q] = value[:, 0:64]
+            second_out[tz * 9 + q] = pltpu.roll(value, 64, 1)[:, 0:64]
 
 
 def reduce_all(p):
     return pl.pallas_call(
         reduce_kernel,
         in_specs=[pl.BlockSpec(memory_space=pltpu.VMEM)],
-        out_specs=pl.BlockSpec(memory_space=pltpu.VMEM),
-        out_shape=jax.ShapeDtypeStruct((2048, 128), BF16),
+        out_specs=[pl.BlockSpec(memory_space=pltpu.VMEM)] * 2,
+        out_shape=[jax.ShapeDtypeStruct((27, 64, 64), F32)] * 2,
         scratch_shapes=[
             pltpu.VMEM((1024, 128), F32),
             pltpu.VMEM((1024, 128), BF16),
-            pltpu.VMEM((3, 256, 128), BF16),
-            pltpu.VMEM((256, 128), F32),
-            pltpu.VMEM((3, 64, 128), F32),
+            pltpu.VMEM((16, 64, 128), BF16),
             pltpu.VMEM((N_Z, 64, 128), BF16),
             pltpu.VMEM((2048, 128), BF16),
-            pltpu.SemaphoreType.DMA((24,)),
-            pltpu.SemaphoreType.DMA((24,)),
+            pltpu.SemaphoreType.DMA((40,)),
+            pltpu.SemaphoreType.DMA((40,)),
         ],
         compiler_params=pltpu.CompilerParams(
             collective_id=2, has_side_effects=True, vmem_limit_bytes=16 * 2**20
         ),
     )(p)
-
-
-def block_weight(w):
-    turned = jnp.transpose(w, (2, 3, 4, 1, 0))[:, :, None, :, :, None, :]
-    same = jnp.eye(2, dtype=w.dtype)[None, None, :, None, None, :, None]
-    return (turned * same).reshape(1152, 384)
 
 
 def halo_places(neighbours):
@@ -515,22 +540,20 @@
 
 
 def per_device(features, cotangent, first_weight, second_weight, counts, neighbours):
-    count = counts[lax.axis_index("group"), lax.axis_index("dev")].reshape(1)
     pos, parity = halo_places(neighbours)
-    w1 = first_weight.reshape(64, 3, 3, 3, 64)
-    w2 = second_weight.reshape(64, 3, 3, 3, 64)
-    wide1, wide2 = block_weight(w1), block_weight(w2)
-    wide_back = block_weight(jnp.transpose(w2[:, ::-1, ::-1, ::-1, :], (4, 1, 2, 3, 0)))
+    w1, w2 = first_weight.transpose(1, 0, 2), second_weight.transpose(1, 0, 2)
     feats = features.reshape(PAIRS, 128, 512)
-    xt, gt, fa, fb = pack(count, feats, cotangent.reshape(PAIRS, 128, 512))
+    xt, gt, fa, fb = pack(counts, feats, cotangent.reshape(PAIRS, 128, 512))
     halos = gather(2, 0, pos, fa, fb)
-    ht, ha, hb, m1 = first_part(count, parity, xt, gt, halos, wide1, wide_back)
+    ht, ha, hb, m1 = first_part(counts, parity, xt, gt, halos, w1, w2)
     halos_h = gather(1, 1, pos, ha, hb)
-    out, p = second_part(count, parity, feats, ht, gt, halos_h, wide2, m1)
-    total = reduce_all(p)
-    total = total[:1728].reshape(3, 3, 3, 64, 2, 64)
-    grads = jnp.transpose(total, (4, 3, 2, 0, 1, 5)).reshape(2, 64, 27, 64).astype(F32)
-    return out.reshape(6, 64, 512), grads[0], grads[1]
+    out, p = second_part(counts, parity, feats, ht, gt, halos_h, w2, m1)
+    first_grad, second_grad = reduce_all(p)
+    return (
+        out.reshape(6, 64, 512),
+        first_grad.transpose(1, 0, 2),
+        second_grad.transpose(1, 0, 2),
+    )
 
 
 def solution(mesh):

time: 190 us -> 162 us (0.85)
  local copies, waits for them, and re-layouts: 18.3 us -> 3.77 us
  other arithmetic: 7.43 us -> 0.73 us
  Pallas kernels: 163 us -> 157 us
    mul x3 -> x0, local copies, waits for them, and re-layouts: 8.35 us -> none  [block_weight(): return (turned * same).reshape(1152, 384)]
    mul x1 -> x0, other arithmetic: 6.64 us -> none  [block_weight(): return (turned * same).reshape(1152, 384)]
    pallas_call x1, Pallas kernels: 31.5 us -> 26.2 us  [reduce_all(): pl.pallas_call(reduce_kernel, in_specs=[pl.BlockSpec(memory_space=pltpu.V...]
    slice x3 -> x0, local copies, waits for them, and re-layouts: 3.96 us -> none  [per_device(): return (out.reshape(6, 64, 512), grads[0], grads[1])]
    unnamed x14 -> x18, local copies, waits for them, and re-layouts: 0.04 us -> 3.77 us
    transpose x2 -> x0, local copies, waits for them, and re-layouts: 2.18 us -> none  [block_weight(): turned = jnp.transpose(w, (2, 3, 4, 1, 0))[:, :, None, :, :, None, :]]
where the time goes in v2:
time: 162 us
  Pallas kernels  157 us (97%)
  local copies, waits for them, and re-layouts  3.77 us (2%)
    pallas_call x2, Pallas kernels, gather(): pl.pallas_call(functools.partial(gather_kernel, fields), in_specs=[pl.Blo...  107 us
    pallas_call x1, Pallas kernels, reduce_all(): pl.pallas_call(reduce_kernel, in_specs=[pl.BlockSpec(memory_space=pltpu.V...  26.2 us
    pallas_call x1, Pallas kernels, first_part(): pl.pallas_call(first_kernel, grid=(PAIRS,), in_specs=[smem, smem, blocked...  10.8 us
    pallas_call x1, Pallas kernels, second_part(): pl.pallas_call(second_kernel, grid=(PAIRS,), in_specs=[smem, smem, blocke...  9.08 us
    unnamed x18, local copies, waits for them, and re-layouts  3.77 us
    pallas_call x1, Pallas kernels, pack(): pl.pallas_call(pack_kernel, grid=(PAIRS,), in_specs=[pl.BlockSpec(memory_...  3.3 us

profile of v2, /device:TPU:1, one launch (start us, length us, event | category | flops | bytes accessed | tf_op | source)
XLA Modules:
  0.0 161.9 jit_solution(8447905624555398772)
XLA Ops:
  0.6 0.7 fusion.8
  1.4 3.3 %shard_map.94 = (bf16[3,512,128]{2,1,0:T(8,128)(2,1)}, bf16[3,512,128]{2,1,0:T(8,128)(2,1)}, bf16[3,6,64,128]{3,2,1,0:T(8,128)(2,1)}, bf16[3,6,64,128]{3,2,1,0:T(8,128)(2,1)}) custom-call(s32[8,32]{1,0:T(8,128)} %count_ref.5, bf16[3,128,512]{2,1,0:T(8,128)(2,1)} %bitcast.9, bf16[3,128,512]{2,1,0:T(8,128)(2,1)} %bitcast.14), custom_call_target="tpu_custom_call" | custom-call | tf_op jit(solution)/shard_map/pallas_call | solution.py:82
  4.7 0.0 copy-start.5
  4.7 1.0 copy-done.5
  5.6 0.0 copy-start.6
  5.6 1.0 copy-done.6
  6.6 0.0 copy-start
  6.6 0.0 copy-start.1
  6.6 0.0 copy-start.3
  6.6 0.0 copy-start.4
  6.6 0.0 copy-start.7
  6.6 69.1 %shard_map.95.hx_ref.hg_ref = bf16[2,6,26,64,128]{4,3,2,1,0:T(8,128)(2,1)S(1)} custom-call(s32[6,26]{1,0:T(8,128)S(1)} %get-tuple-element.27.pos_ref, bf16[3,6,64,128]{3,2,1,0:T(8,128)(2,1)S(1)} %copy-done.5, bf16[3,6,64,128]{3,2,1,0:T(8,128)(2,1)S(1)} %copy-done.6), custom_call_target="tpu_custom_call" | custom-call | tf_op jit(solution)/shard_map/pallas_call | solution.py:211
  75.8 0.0 copy-done
  75.8 0.0 copy-done.1
  75.8 0.0 copy-done.3
  75.8 0.0 copy-done.4
  75.8 0.0 copy-done.7
  75.8 10.8 %shard_map.96 = (bf16[3,512,128]{2,1,0:T(8,128)(2,1)S(1)}, bf16[3,3,64,128]{3,2,1,0:T(8,128)(2,1)S(1)}, bf16[3,3,64,128]{3,2,1,0:T(8,128)(2,1)S(1)}, f32[384,1152]{1,0:T(8,128)S(1)}) custom-call(s32[8,32]{1,0:T(8,128)S(1)} %copy-done.7, s32[6,26]{1,0:T(8,128)S(1)} %get-tuple-element.28.par_ref, bf16[3,512,128]{2,1,0:T(8,128)(2,1)S(1)} %copy-done.4, ...), custom_call_target="tpu_custom_call" | custom-call | tf_op jit(solution)/shard_map/pallas_call | solution.py:365
  86.6 0.0 copy-start.2
  86.7 38.1 %shard_map.97.hh_ref = bf16[1,6,26,64,128]{4,3,2,1,0:T(8,128)(2,1)S(1)} custom-call(s32[6,26]{1,0:T(8,128)S(1)} %get-tuple-element.27.pos_ref, bf16[3,3,64,128]{3,2,1,0:T(8,128)(2,1)S(1)} %get-tuple-element.20.fa_ref, bf16[3,3,64,128]{3,2,1,0:T(8,128)(2,1)S(1)} %get-tuple-element.21.fb_ref), custom_call_target="tpu_custom_call" | custom-call | tf_op jit(solution)/shard_map/pallas_call | solution.py:211
  124.7 0.0 copy-done.2
  124.7 9.1 %shard_map.98 = (bf16[3,128,512]{2,1,0:T(8,128)(2,1)}, f32[2048,128]{1,0:T(8,128)S(1)}) custom-call(s32[8,32]{1,0:T(8,128)S(1)} %copy-done.7, s32[6,26]{1,0:T(8,128)S(1)} %get-tuple-element.28.par_ref, bf16[3,128,512]{2,1,0:T(8,128)(2,1)S(1)} %bitcast.10, bf16[3,512,128]{2,1,0:T(8,128)(2,1)S(1)} %get-tuple-element.19.h_ref, ...), custom_call_target="tpu_custom_call" | custom-call | tf_op jit(solution)/shard_map/pallas_call | solution.py:429
  133.8 26.2 %shard_map.99 = (f32[27,64,64]{2,1,0:T(8,128)S(1)}, f32[27,64,64]{2,1,0:T(8,128)S(1)}) custom-call(f32[2048,128]{1,0:T(8,128)S(1)} %get-tuple-element.24.p_ref), custom_call_target="tpu_custom_call" | custom-call | tf_op jit(solution)/shard_map/pallas_call | solution.py:512
  160.1 0.9 copy.12
  161.0 0.9 copy.13
Async XLA Ops:
  4.7 1.0 copy-start.5
  5.6 1.0 copy-start.6
  6.6 69.2 %copy-start = (bf16[64,27,64]{2,0,1:T(8,128)(2,1)S(1)}, bf16[64,27,64]{2,0,1:T(8,128)(2,1)}, u32[]{:S(2)}) copy-start(bf16[64,27,64]{2,0,1:T(8,128)(2,1)} %param.10) | copy-start | bytes 663556
  6.6 69.2 %copy-start.1 = (bf16[3,512,128]{2,1,0:T(8,128)(2,1)S(1)}, bf16[3,512,128]{2,1,0:T(8,128)(2,1)}, u32[]{:S(2)}) copy-start(bf16[3,512,128]{2,1,0:T(8,128)(2,1)} %get-tuple-element.16.g_ref) | copy-start | bytes 1179652
  6.6 69.2 %copy-start.3 = (bf16[64,27,64]{2,0,1:T(8,128)(2,1)S(1)}, bf16[64,27,64]{2,0,1:T(8,128)(2,1)}, u32[]{:S(2)}) copy-start(bf16[64,27,64]{2,0,1:T(8,128)(2,1)} %param.9) | copy-start | bytes 663556
  6.6 69.2 %copy-start.4 = (bf16[3,512,128]{2,1,0:T(8,128)(2,1)S(1)}, bf16[3,512,128]{2,1,0:T(8,128)(2,1)}, u32[]{:S(2)}) copy-start(bf16[3,512,128]{2,1,0:T(8,128)(2,1)} %get-tuple-element.15.x_ref) | copy-start | bytes 1179652
  6.6 69.2 %copy-start.7 = (s32[8,32]{1,0:T(8,128)S(1)}, s32[8,32]{1,0:T(8,128)}, u32[]{:S(2)}) copy-start(s32[8,32]{1,0:T(8,128)} %count_ref.5) | copy-start | bytes 3076
  86.6 38.1 %copy-start.2 = (bf16[6,64,512]{2,1,0:T(8,128)(2,1)S(1)}, bf16[6,64,512]{2,1,0:T(8,128)(2,1)}, u32[]{:S(2)}) copy-start(bf16[6,64,512]{2,1,0:T(8,128)(2,1)} %param.7) | copy-start | bytes 1179652

commit v3 on v2

v3 whole, which is shorter than its diff:
```python
import functools

import jax
import jax.numpy as jnp
import numpy as np
from jax import lax
from jax.experimental import pallas as pl
from jax.experimental.pallas import tpu as pltpu
from jax.sharding import PartitionSpec as P

MESH = pl.DeviceIdType.MESH
F32 = jnp.float32
BF16 = jnp.bfloat16
N_Z, N_Y, N_X = 8, 4, 4
PAIRS = 3
DIRECTIONS = [
    (dz, dy, dx)
    for dz in (-1, 0, 1)
    for dy in (-1, 0, 1)
    for dx in (-1, 0, 1)
    if (dz, dy, dx) != (0, 0, 0)
]


def face_of(direction):
    dz, dy, dx = direction
    if dz != 0:
        return (0 if dz == 1 else 1), 2
    if dx != 0:
        return (0 if dx == 1 else 1), 0
    return (0 if dy == 1 else 1), 1


def place():
    d = lax.axis_index("dev")
    return lax.axis_index("group"), d // 8, (d // 2) % 4, d % 2


def device(g, y, x, c):
    return (g, (y * 4 + x) * 2 + c)


class Gather:
    def __init__(self, field, bufs, zsrc, send, recv, started):
        self.field, self.bufs, self.zsrc = field, bufs, zsrc
        self.send, self.recv, self.started = send, recv, started
        self.g, self.y, self.x, self.c = place()
        self.mine = ((self.x, self.y), (self.y, self.x))
        self.axes = (("x", "y"), ("y", "x"))
        self.made = [dict(), dict()]

    def moved(self, axis, step):
        if axis == "x":
            return device(self.g, self.y, (self.x + step + N_X) % N_X, self.c)
        return device(self.g, (self.y + step + N_Y) % N_Y, self.x, self.c)

    def at(self, half, first):
        return ((self.c * 4 + self.mine[half][1]) * 4 + first) * 3

    def own(self, half):
        return self.at(half, self.mine[half][0])

    def row(self, half, step):
        return pl.ds((self.c * 4 + (self.mine[half][1] + step + 4) % 4) * 12, 12)

    def copy(self, half, number, src, dst, target):
        one = pltpu.make_async_remote_copy(
            src_ref=src,
            dst_ref=dst,
            send_sem=self.send.at[self.field, half, number],
            recv_sem=self.recv.at[self.field, half, number],
            device_id=target,
            device_id_type=MESH,
        )
        one.start()
        self.started.append(one)
        self.made[half][number] = one

    def same(self, half, number, index, target):
        part = self.bufs[half].at[index]
        self.copy(half, number, part, part, target)

    def came(self, half, *numbers):
        for number in numbers:
            self.made[half][number].wait_recv()

    def sibling(self):
        return device(self.g, self.y, self.x, 1 - self.c)

    def write(self, pair, value, scratch):
        scratch[...] = value
        cube = value.reshape(8, 8, 8, 128)
        for half, edge in ((0, 0), (1, 7)):
            at = self.own(half) + pair
            out = self.bufs[half]
            out[at, 0] = scratch[pl.ds(edge, 64, stride=8), :].astype(BF16)
            out[at, 1] = cube[:, edge].reshape(64, 128).astype(BF16)
            self.zsrc[half, pair, 0] = value[edge * 64:edge * 64 + 64].astype(BF16)

    def clear(self):
        for half in range(2):
            self.bufs[half][96:97] = jnp.zeros((1, 3, 64, 128), BF16)

    def layers(self):
        for half, step in ((0, N_Z - 1), (1, 1)):
            target = device((self.g + step) % N_Z, self.y, self.x, self.c)
            dst = self.bufs[half].at[pl.ds(self.own(half), 3), pl.ds(2, 1)]
            self.copy(half, 0, self.zsrc.at[half], dst, target)

    def step0(self):
        for half in range(2):
            self.came(half, 0)
            for number, step in ((1, 1), (2, -1)):
                block = pl.ds(self.own(half), 3)
                self.same(half, number, block, self.moved(self.axes[half][0], step))

    def step1(self):
        for number, step, rows in ((3, 1, pl.ds(0, 32)), (4, -1, pl.ds(32, 32))):
            for half in range(2):
                self.came(half, number - 2)
                block = pl.ds(self.at(half, (self.mine[half][0] - step + 4) % 4), 3)
                index = (block, slice(None), rows)
                self.same(half, number, index, self.moved(self.axes[half][0], step))

    def step2(self):
        for half in range(2):
            self.came(half, 3, 4)
            for number, step in ((5, 1), (6, -1)):
                target = self.moved(self.axes[half][1], step)
                self.same(half, number, self.row(half, 0), target)
            self.same(half, 9, self.row(half, 0), self.sibling())

    def step3(self):
        for number, step, rows in ((7, 1, pl.ds(0, 32)), (8, -1, pl.ds(32, 32))):
            for half in range(2):
                self.came(half, number - 2)
                index = (self.row(half, -step), slice(None), rows)
                self.same(half, number, index, self.moved(self.axes[half][1], step))
                self.same(half, number + 3, self.row(half, -step), self.sibling())

    def step4(self):
        for number, rows in ((7, pl.ds(0, 32)), (8, pl.ds(32, 32))):
            for half in range(2):
                self.came(half, number)
                index = (self.row(half, 2), slice(None), rows)
                self.same(half, number + 5, index, self.sibling())

    def step5(self):
        for half in range(2):
            self.came(half, 9, 10, 11, 12, 13)


def build_cube(cube, own, bufs, pos_ref, par_ref, pair):
    low = lax.broadcasted_iota(jnp.int32, (1, 128), 1) < 64
    cube[1:9, 1:9, 8:16, :] = own.reshape(8, 8, 8, 128)
    for k, (dz, dy, dx) in enumerate(DIRECTIONS):
        half, face = face_of((dz, dy, dx))
        if dz != 0 and dy != 0:
            start, count = (0, 16) if dy == 1 else (48, 16)
        else:
            start, count = 0, 64
        picked = []
        for s in range(2):
            at = pos_ref[2 * pair + s, k]
            value = bufs[half][at, face, start:start + count].astype(F32)
            turned = pltpu.roll(value, 64, 1)
            picked.append(jnp.where(par_ref[2 * pair + s, k] == s, value, turned))
        piece = jnp.where(low, picked[0], picked[1])
        if count == 16:
            piece = piece[0:8] if dy == 1 else piece[8:16]
        zz = {-1: 0, 1: 9}.get(dz)
        yy = {-1: 0, 1: 9}.get(dy)
        if dx == 0:
            if dz == 0:
                cube[1:9, yy, 8:16, :] = piece.reshape(8, 8, 128)
            elif dy == 0:
                cube[zz, 1:9, 8:16, :] = piece.reshape(8, 8, 128)
            else:
                cube[zz, yy, 8:16, :] = piece
            continue
        sub = 7 if dx == -1 else 16
        edge_x = 7 if dx == -1 else 0
        edge_y = 7 if dy == -1 else 0
        if dz == 0 and dy == 0:
            rows = [(z + 1, q + 1, z * 8 + q) for z in range(8) for q in range(8)]
        elif dz == 0:
            rows = [(z + 1, yy, z * 8 + edge_y) for z in range(8)]
        elif dy == 0:
            rows = [(zz, q + 1, q * 8 + edge_x) for q in range(8)]
        else:
            rows = [(zz, yy, edge_x)]
        for a, b, r in rows:
            cube[a, b, sub:sub + 1, :] = piece[r:r + 1]


def stack_taps(cube, taps, pair):
    for ty in range(3):
        for tx in range(3):
            part = cube[:, ty:ty + 8, 7 + tx:15 + tx, :].reshape(640, 128)
            column = (ty * 3 + tx) * 128
            taps[pair, :, column:column + 128] = part.astype(BF16)


def tap_of(w_ref, tap):
    value = w_ref[tap].astype(F32)
    return jnp.concatenate([value, value], axis=1)


def widen(w_ref, wide, backward):
    low = lax.broadcasted_iota(jnp.int32, (1, 128), 1) < 64
    for tz in range(3):
        for q in range(9):
            tap = tz * 9 + q
            value = tap_of(w_ref, 26 - tap if backward else tap)
            a, b = (q, tz) if backward else (tz, q)
            lanes = pl.ds(b * 128, 128)
            wide[pl.ds(a * 128, 64), lanes] = jnp.where(low, value, 0.0).astype(BF16)
            wide[pl.ds(a * 128 + 64, 64), lanes] = jnp.where(low, 0.0, value).astype(BF16)


def convolve(taps, wide, backward=False):
    contract = (((1,), (0 if backward else 1,)), ((), ()))
    wide = lax.dot_general(taps, wide[...], contract, preferred_element_type=F32)
    return wide[0:512, 0:128] + wide[64:576, 128:256] + wide[128:640, 256:384]


def spread(wide_g, pair, value):
    for tz in range(3):
        wide_g[pair, tz * 64:tz * 64 + 512, tz * 128:tz * 128 + 128] = value


def outer(wide_g, taps):
    return lax.dot_general(
        wide_g[...].reshape(PAIRS * 640, 384),
        taps[...].reshape(PAIRS * 640, 1152),
        (((0,), (0,)), ((), ())),
        preferred_element_type=F32,
    )


def block_kernel(count_ref, pos_ref, par_ref, f_ref, c_ref, w_ref, v_ref,
                 o_out, first_out, second_out,
                 xa, xb, ga, gb, ha, hb, zx, zg, zh, xs, gs, hs, scratch, cube, taps,
                 taps_g, wide_g, wide_w, wide_b, wide_v, product, p_sum,
                 r1, a1, r2, r4, whole, send, recv, send_sum, recv_sum):
    g, y, x, c = place()
    sibling = device(g, y, x, 1 - c)
    layer = [
        ((y + ky) % N_Y, (x + kx) % N_X, ky * N_X + kx)
        for ky in range(N_Y)
        for kx in range(N_X)
        if (ky, kx) != (0, 0)
    ]
    zs = [device((g + k) % N_Z, y, x, c) for k in range(1, N_Z)]
    partners = [sibling] + [device(g, yy, xx, c) for yy, xx, _ in layer] + zs
    barrier = pltpu.get_barrier_semaphore()
    for partner in partners:
        pl.semaphore_signal(barrier, inc=1, device_id=partner, device_id_type=MESH)

    count = count_ref[g, lax.axis_index("dev")]
    low = lax.broadcasted_iota(jnp.int32, (1, 128), 1) < 64
    started = []
    gx = Gather(0, (xa, xb), zx, send, recv, started)
    gg = Gather(1, (ga, gb), zg, send, recv, started)
    gh = Gather(2, (ha, hb), zh, send, recv, started)

    def live(pair):
        return jnp.where(low, 2 * pair, 2 * pair + 1) < count

    def over_pairs(body):
        def step(pair, carry):
            body(pair)
            return carry

        lax.fori_loop(0, PAIRS, step, 0)

    def pack_x(pair):
        value = f_ref[pair].astype(F32).T
        xs[pair] = value.astype(BF16)
        gx.write(pair, value, scratch)

    def pack_g(pair):
        value = jnp.where(live(pair), c_ref[pair].astype(F32).T, 0.0)
        gs[pair] = value.astype(BF16)
        gg.write(pair, value, scratch)

    def forward(pair):
        build_cube(cube, xs[pair].astype(F32), gx.bufs, pos_ref, par_ref, pair)
        stack_taps(cube, taps, pair)
        first = convolve(taps[pair], wide_w)
        hidden = jnp.where(live(pair), jnp.maximum(first, 0.0), 0.0)
        hidden = hidden.astype(BF16).astype(F32)
        hs[pair] = hidden.astype(BF16)
        gh.write(pair, hidden, scratch)

    def backward(pair):
        build_cube(cube, gs[pair].astype(F32), gg.bufs, pos_ref, par_ref, pair)
        stack_taps(cube, taps_g, 0)
        back = convolve(taps_g[0], wide_b, True)
        grad = jnp.where(hs[pair].astype(F32) > 0, back, 0.0)
        spread(wide_g, pair, grad.astype(BF16))

    def stack_h(pair):
        build_cube(cube, hs[pair].astype(F32), gh.bufs, pos_ref, par_ref, pair)
        stack_taps(cube, taps, pair)
        spread(wide_g, pair, gs[pair])

    def finish(pair):
        second = convolve(taps[pair], wide_v)
        lane = lax.broadcasted_iota(jnp.int32, (128, 1), 0)
        slot = jnp.where(lane < 64, 2 * pair, 2 * pair + 1)
        result = f_ref[pair].astype(F32) + second.T
        o_out[pair] = jnp.where(slot < count, result, 0.0).astype(BF16)

    over_pairs(pack_x)
    pl.semaphore_wait(barrier, len(partners))
    gx.layers()
    over_pairs(pack_g)
    gg.layers()
    gx.step0()
    for one in (gx, gg, gh):
        one.clear()
    widen(w_ref, wide_w, False)
    gx.step1()
    widen(v_ref, wide_b, True)
    gx.step2()
    widen(v_ref, wide_v, False)
    wide_g[...] = jnp.zeros((PAIRS, 640, 384), BF16)
    gx.step3()
    gg.step0()
    gx.step4()
    gg.step1()
    gx.step5()
    over_pairs(forward)
    gh.layers()
    gg.step2()
    gh.step0()
    gh.step1()
    gh.step2()
    gg.step3()
    gg.step4()
    gg.step5()
    over_pairs(backward)
    gh.step3()
    product[...] = outer(wide_g, taps)
    for q in range(9):
        for tz in range(3):
            even, odd = pl.ds(tz * 128, 64), pl.ds(tz * 128 + 64, 64)
            lanes = pl.ds(q * 128, 128)
            one = product[even, lanes] + pltpu.roll(product[odd, lanes], 64, 1)
            p_sum[pl.ds((q * 3 + tz) * 64, 64), :] = one
    p_sum[1728:2048, :] = jnp.zeros((320, 128), F32)
    gh.step4()
    gh.step5()
    over_pairs(stack_h)
    product[...] = outer(wide_g, taps)
    for q in range(9):
        for tz in range(3):
            even, odd = pl.ds(tz * 128, 64), pl.ds(tz * 128 + 64, 64)
            lanes = pl.ds(q * 128, 128)
            rows = pl.ds((q * 3 + tz) * 64, 64)
            two = pltpu.roll(product[even, lanes], 64, 1) + product[odd, lanes]
            p_sum[rows, :] = jnp.where(low, p_sum[rows, :], two)

    used = [0]

    def copy(src, dst, target):
        number = used[0]
        used[0] += 1
        one = pltpu.make_async_remote_copy(
            src_ref=src, dst_ref=dst, send_sem=send_sum.at[number],
            recv_sem=recv_sum.at[number], device_id=target, device_id_type=MESH,
        )
        one.start()
        return one

    one = copy(p_sum.at[pl.ds((1 - c) * 1024, 1024)], r1, sibling)
    finish(0)
    one.wait()
    a1[...] = (p_sum[pl.ds(c * 1024, 1024)] + r1[...]).astype(BF16)

    made = [
        copy(a1.at[pl.ds((yy * N_X + xx) * 64, 64)], r2.at[k], device(g, yy, xx, c))
        for yy, xx, k in layer
    ]
    finish(1)
    for one in made:
        one.wait()
    at = y * N_X + x
    part = a1[pl.ds(at * 64, 64)].astype(F32)
    for k in range(1, 16):
        part = part + r2[k].astype(F32)
    r4[g] = part.astype(BF16)

    made = [copy(r4.at[g], r4.at[g], target) for target in zs]
    finish(2)
    for one in made:
        one.wait()
    part = r4[0].astype(F32)
    for k in range(1, N_Z):
        part = part + r4[k].astype(F32)
    rows = pl.ds(c * 1024 + at * 64, 64)
    whole[rows] = part.astype(BF16)

    made = [
        copy(whole.at[rows], whole.at[rows], device(g, yy, xx, c)) for yy, xx, _ in layer
    ]
    for one in made:
        one.wait()
    half = pl.ds(c * 1024, 1024)
    copy(whole.at[half], whole.at[half], sibling).wait()
    for q in range(9):
        for tz in range(3):
            value = whole[pl.ds((q * 3 + tz) * 64, 64)].astype(F32)
            first_out[tz * 9 + q] = value[:, 0:64]
            second_out[tz * 9 + q] = pltpu.roll(value, 64, 1)[:, 0:64]
    for one in started:
        one.wait_send()


def block(counts, pos, parity, features, cotangent, w, v):
    smem, vmem = pl.BlockSpec(memory_space=pltpu.SMEM), pl.BlockSpec(memory_space=pltpu.VMEM)
    return pl.pallas_call(
        block_kernel,
        in_specs=[smem] * 3 + [vmem] * 4,
        out_specs=[vmem] * 3,
        out_shape=[
            jax.ShapeDtypeStruct((PAIRS, 128, 512), BF16),
            jax.ShapeDtypeStruct((27, 64, 64), F32),
            jax.ShapeDtypeStruct((27, 64, 64), F32),
        ],
        scratch_shapes=[pltpu.VMEM((97, 3, 64, 128), BF16)] * 6
        + [pltpu.VMEM((2, PAIRS, 1, 64, 128), BF16)] * 3
        + [pltpu.VMEM((PAIRS, 512, 128), BF16)] * 3
        + [
            pltpu.VMEM((512, 128), F32),
            pltpu.VMEM((10, 10, 24, 128), F32),
            pltpu.VMEM((PAIRS, 640, 1152), BF16),
            pltpu.VMEM((1, 640, 1152), BF16),
            pltpu.VMEM((PAIRS, 640, 384), BF16),
            pltpu.VMEM((384, 1152), BF16),
            pltpu.VMEM((1152, 384), BF16),
            pltpu.VMEM((384, 1152), BF16),
            pltpu.VMEM((384, 1152), F32),
            pltpu.VMEM((2048, 128), F32),
            pltpu.VMEM((1024, 128), F32),
            pltpu.VMEM((1024, 128), BF16),
            pltpu.VMEM((16, 64, 128), BF16),
            pltpu.VMEM((N_Z, 64, 128), BF16),
            pltpu.VMEM((2048, 128), BF16),
            pltpu.SemaphoreType.DMA((3, 2, 14)),
            pltpu.SemaphoreType.DMA((3, 2, 14)),
            pltpu.SemaphoreType.DMA((40,)),
            pltpu.SemaphoreType.DMA((40,)),
        ],
        compiler_params=pltpu.CompilerParams(
            collective_id=0, has_side_effects=True, vmem_limit_bytes=62 * 2**20
        ),
    )(counts, pos, parity, features, cotangent, w, v)


def halo_places(neighbours):
    halves = jnp.asarray(np.array([face_of(d)[0] for d in DIRECTIONS], np.int32))[None, :]
    dev = neighbours // 6 % 32
    y, x, c = dev // 8, dev // 2 % 4, dev % 2
    first = jnp.where(halves == 0, x, y)
    second = jnp.where(halves == 0, y, x)
    pos = ((c * 4 + second) * 4 + first) * 3 + neighbours % 6 // 2
    return jnp.where(neighbours >= 0, pos, 96).astype(jnp.int32), neighbours % 2


def per_device(features, cotangent, first_weight, second_weight, counts, neighbours):
    pos, parity = halo_places(neighbours)
    out, first_grad, second_grad = block(
        counts,
        pos,
        parity,
        features.reshape(PAIRS, 128, 512),
        cotangent.reshape(PAIRS, 128, 512),
        first_weight.transpose(1, 0, 2),
        second_weight.transpose(1, 0, 2),
    )
    return (
        out.reshape(6, 64, 512),
        first_grad.transpose(1, 0, 2),
        second_grad.transpose(1, 0, 2),
    )


def solution(mesh):
    placed = (
        P(("group", "dev"), None, None),
        P(("group", "dev"), None, None),
        P(),
        P(),
        P(),
        P(("group", "dev"), None),
    )
    return jax.shard_map(
        per_device,
        mesh=mesh,
        in_specs=placed,
        out_specs=(P(("group", "dev"), None, None), P(), P()),
        check_vma=False,
    )
```

time: 162 us -> 147 us (0.907)
  Pallas kernels: 157 us -> 140 us
  local copies, waits for them, and re-layouts: 3.77 us -> 5.62 us
    pallas_call x6 -> x1, Pallas kernels: 157 us -> 140 us  [block(): pl.pallas_call(block_kernel, in_specs=[smem] * 3 + [vmem] * 4, out_specs=...]
    unnamed x18 -> x9, local copies, waits for them, and re-layouts: 3.77 us -> 5.62 us
where the time goes in v3:
time: 147 us; the launch traced here: 146 us
  Pallas kernels  140 us (95%)
  local copies, waits for them, and re-layouts  5.62 us (4%)
    pallas_call x1, Pallas kernels, block(): pl.pallas_call(block_kernel, in_specs=[smem] * 3 + [vmem] * 4, out_specs=...  140 us
    unnamed x9, local copies, waits for them, and re-layouts  5.62 us

profile of v3, /device:TPU:1, one launch (start us, length us, event | category | flops | bytes accessed | tf_op | source)
XLA Modules:
  0.0 146.4 jit_solution(3951023848260262188)
XLA Ops:
  0.6 0.0 copy-start.1
  0.6 0.0 copy-start.2
  0.7 0.7 copy-done.1
  1.3 0.0 copy-done.2
  1.3 0.6 add_select_fusion
  2.0 139.5 %shard_map.94 = (bf16[3,128,512]{2,1,0:T(8,128)(2,1)}, f32[27,64,64]{2,1,0:T(8,128)}, f32[27,64,64]{2,1,0:T(8,128)}) custom-call(s32[8,32]{1,0:T(8,128)} %count_ref.1, s32[6,26]{1,0:T(8,128)} %get-tuple-element.10.pos_ref, s32[6,26]{1,0:T(8,128)} %get-tuple-element.9.par_ref, bf16[3,128,512]{2,1,0:T(8,128)(2,1)} %bitcast.12, bf16[3,128,512]{2,1,0:T(8,128)(2,1)} %bitcast.13, ...), custom_call_target="tpu_custom_call" | custom-call | tf_op jit(solution)/shard_map/pallas_call | solution.py:423
  141.5 1.8 %copy.13 = bf16[6,64,512]{2,1,0:T(8,128)(2,1)} copy(bf16[6,64,512]{2,1,0:T(8,128)(2,1)} %bitcast.11) | data formatting | bytes 786432
  143.3 0.0 copy-start
  143.3 2.3 %copy.14 = f32[64,27,64]{2,0,1:T(8,128)} copy(f32[64,27,64]{2,0,1:T(8,128)} %bitcast.8) | data formatting | bytes 884736
  145.5 0.0 copy-done
  145.5 0.9 copy.15
Async XLA Ops:
  0.6 0.7 copy-start.1
  0.6 0.7 copy-start.2
  143.3 2.3 %copy-start = (f32[27,64,64]{2,1,0:T(8,128)S(1)}, f32[27,64,64]{2,1,0:T(8,128)}, u32[]{:S(2)}) copy-start(f32[27,64,64]{2,1,0:T(8,128)} %get-tuple-element.8) | copy-start | bytes 1327108

commit v4 on v3

--- a/solution.py
+++ b/solution.py
@@ -41,116 +41,125 @@
 
 
 class Gather:
-    def __init__(self, field, bufs, zsrc, send, recv, started):
-        self.field, self.bufs, self.zsrc = field, bufs, zsrc
+    def __init__(self, field, cap, list_ref, rows, line, src, send, recv, started):
+        self.field, self.cap, self.list_ref = field, cap, list_ref
+        self.rows, self.line, self.src = rows, line, src
         self.send, self.recv, self.started = send, recv, started
         self.g, self.y, self.x, self.c = place()
-        self.mine = ((self.x, self.y), (self.y, self.x))
-        self.axes = (("x", "y"), ("y", "x"))
-        self.made = [dict(), dict()]
-
-    def moved(self, axis, step):
-        if axis == "x":
-            return device(self.g, self.y, (self.x + step + N_X) % N_X, self.c)
-        return device(self.g, (self.y + step + N_Y) % N_Y, self.x, self.c)
-
-    def at(self, half, first):
-        return ((self.c * 4 + self.mine[half][1]) * 4 + first) * 3
-
-    def own(self, half):
-        return self.at(half, self.mine[half][0])
-
-    def row(self, half, step):
-        return pl.ds((self.c * 4 + (self.mine[half][1] + step + 4) % 4) * 12, 12)
-
-    def copy(self, half, number, src, dst, target):
-        one = pltpu.make_async_remote_copy(
+        self.i = self.first(self.c)
+        self.j = self.first(1 - self.c)
+        self.made = dict()
+
+    def first(self, half):
+        return self.x * (1 - half) + self.y * half
+
+    def moved(self, first, step):
+        along_y = self.c if first else 1 - self.c
+        y = (self.y + step * along_y + N_Y) % N_Y
+        x = (self.x + step * (1 - along_y) + N_X) % N_X
+        return device(self.g, y, x, self.c)
+
+    def row(self, step):
+        return pl.ds((self.j + step + 4) % 4 * 24, self.cap)
+
+    def block(self, step):
+        return pl.ds((self.i + step + 4) % 4 * 6, 6)
+
+    def sibling(self):
+        return device(self.g, self.y, self.x, 1 - self.c)
+
+    def describe(self, number, came, src, dst, target):
+        return pltpu.make_async_remote_copy(
             src_ref=src,
             dst_ref=dst,
-            send_sem=self.send.at[self.field, half, number],
-            recv_sem=self.recv.at[self.field, half, number],
+            send_sem=self.send.at[self.field, number],
+            recv_sem=self.recv.at[self.field, came],
             device_id=target,
             device_id_type=MESH,
         )
+
+    def copy(self, number, came, src, dst, target):
+        one = self.describe(number, came, src, dst, target)
         one.start()
         self.started.append(one)
-        self.made[half][number] = one
-
-    def same(self, half, number, index, target):
-        part = self.bufs[half].at[index]
-        self.copy(half, number, part, part, target)
-
-    def came(self, half, *numbers):
+        self.made[number] = one
+
+    def same(self, number, part, target):
+        self.copy(number, number, part, part, target)
+
+    def came(self, *numbers):
         for number in numbers:
-            self.made[half][number].wait_recv()
-
-    def sibling(self):
-        return device(self.g, self.y, self.x, 1 - self.c)
+            self.made[number].wait_recv()
 
     def write(self, pair, value, scratch):
         scratch[...] = value
         cube = value.reshape(8, 8, 8, 128)
         for half, edge in ((0, 0), (1, 7)):
-            at = self.own(half) + pair
-            out = self.bufs[half]
-            out[at, 0] = scratch[pl.ds(edge, 64, stride=8), :].astype(BF16)
-            out[at, 1] = cube[:, edge].reshape(64, 128).astype(BF16)
-            self.zsrc[half, pair, 0] = value[edge * 64:edge * 64 + 64].astype(BF16)
+            self.src[half, pair, 0] = scratch[pl.ds(edge, 64, stride=8), :].astype(BF16)
+            self.src[half, pair, 1] = cube[:, edge].reshape(64, 128).astype(BF16)
+            self.src[half, pair, 2] = value[edge * 64:edge * 64 + 64].astype(BF16)
 
     def clear(self):
         for half in range(2):
-            self.bufs[half][96:97] = jnp.zeros((1, 3, 64, 128), BF16)
-
-    def layers(self):
+            self.rows[half, 96:97] = jnp.zeros((1, 3, 64, 128), BF16)
+
+    def begin(self):
+        sides, plane, c = pl.ds(0, 2), pl.ds(2, 1), self.c
         for half, step in ((0, N_Z - 1), (1, 1)):
-            target = device((self.g + step) % N_Z, self.y, self.x, self.c)
-            dst = self.bufs[half].at[pl.ds(self.own(half), 3), pl.ds(2, 1)]
-            self.copy(half, 0, self.zsrc.at[half], dst, target)
+            target = device((self.g + step) % N_Z, self.y, self.x, half)
+            dst = self.line.at[pl.ds(self.first(half) * 6 + c * 3, 3), plane]
+            self.copy(1 + half, 1 + c, self.src.at[half, :, plane], dst, target)
+        dst = self.line.at[pl.ds(self.first(1 - c) * 6 + c * 3, 3), sides]
+        self.copy(0, 0, self.src.at[1 - c, :, sides], dst, self.sibling())
+        self.line[pl.ds(self.i * 6 + c * 3, 3), 0:2] = self.src[c, :, 0:2]
 
     def step0(self):
-        for half in range(2):
-            self.came(half, 0)
-            for number, step in ((1, 1), (2, -1)):
-                block = pl.ds(self.own(half), 3)
-                self.same(half, number, block, self.moved(self.axes[half][0], step))
+        self.came(0)
+        part = self.line.at[pl.ds(0, 3), pl.ds(2, 1)]
+        for core in range(2):
+            self.describe(1, 1 + core, part, part, self.sibling()).wait_recv()
+        for number, step in ((3, 1), (4, -1)):
+            self.same(number, self.line.at[self.block(0)], self.moved(True, step))
 
     def step1(self):
-        for number, step, rows in ((3, 1, pl.ds(0, 32)), (4, -1, pl.ds(32, 32))):
-            for half in range(2):
-                self.came(half, number - 2)
-                block = pl.ds(self.at(half, (self.mine[half][0] - step + 4) % 4), 3)
-                index = (block, slice(None), rows)
-                self.same(half, number, index, self.moved(self.axes[half][0], step))
+        for number, step, rows in ((5, 1, pl.ds(0, 32)), (6, -1, pl.ds(32, 32))):
+            self.came(number - 2)
+            part = self.line.at[self.block(-step), :, rows]
+            self.same(number, part, self.moved(True, step))
 
     def step2(self):
-        for half in range(2):
-            self.came(half, 3, 4)
-            for number, step in ((5, 1), (6, -1)):
-                target = self.moved(self.axes[half][1], step)
-                self.same(half, number, self.row(half, 0), target)
-            self.same(half, 9, self.row(half, 0), self.sibling())
+        self.came(5, 6)
+
+        def one(k, carry):
+            at = self.j * 24 + k
+            self.rows[self.c, at, 0:2] = self.line[self.list_ref[0, k], 0:2]
+            self.rows[self.c, at, 2:3] = self.line[self.list_ref[1, k], 2:3]
+            return carry
+
+        lax.fori_loop(0, self.cap, one, 0)
+        part = self.rows.at[self.c, self.row(0)]
+        for number, step in ((7, 1), (8, -1)):
+            self.same(number, part, self.moved(False, step))
+        self.same(11, part, self.sibling())
 
     def step3(self):
-        for number, step, rows in ((7, 1, pl.ds(0, 32)), (8, -1, pl.ds(32, 32))):
-            for half in range(2):
-                self.came(half, number - 2)
-                index = (self.row(half, -step), slice(None), rows)
-                self.same(half, number, index, self.moved(self.axes[half][1], step))
-                self.same(half, number + 3, self.row(half, -step), self.sibling())
+        for number, step, rows in ((9, 1, pl.ds(0, 32)), (10, -1, pl.ds(32, 32))):
+            self.came(number - 2)
+            part = self.rows.at[self.c, self.row(-step), :, rows]
+            self.same(number, part, self.moved(False, step))
+            self.same(number + 3, self.rows.at[self.c, self.row(-step)], self.sibling())
 
     def step4(self):
-        for number, rows in ((7, pl.ds(0, 32)), (8, pl.ds(32, 32))):
-            for half in range(2):
-                self.came(half, number)
-                index = (self.row(half, 2), slice(None), rows)
-                self.same(half, number + 5, index, self.sibling())
+        for number, rows in ((9, pl.ds(0, 32)), (10, pl.ds(32, 32))):
+            self.came(number)
+            part = self.rows.at[self.c, self.row(2), :, rows]
+            self.same(number + 5, part, self.sibling())
 
     def step5(self):
-        for half in range(2):
-            self.came(half, 9, 10, 11, 12, 13)
-
-
-def build_cube(cube, own, bufs, pos_ref, par_ref, pair):
+        self.came(11, 12, 13, 14, 15)
+
+
+def build_cube(cube, own, rows_ref, pos_ref, par_ref, pair):
     low = lax.broadcasted_iota(jnp.int32, (1, 128), 1) < 64
     cube[1:9, 1:9, 8:16, :] = own.reshape(8, 8, 8, 128)
     for k, (dz, dy, dx) in enumerate(DIRECTIONS):
@@ -162,7 +171,7 @@
         picked = []
         for s in range(2):
             at = pos_ref[2 * pair + s, k]
-            value = bufs[half][at, face, start:start + count].astype(F32)
+            value = rows_ref[half, at, face, start:start + count].astype(F32)
             turned = pltpu.roll(value, 64, 1)
             picked.append(jnp.where(par_ref[2 * pair + s, k] == s, value, turned))
         piece = jnp.where(low, picked[0], picked[1])
@@ -238,9 +247,9 @@
     )
 
 
-def block_kernel(count_ref, pos_ref, par_ref, f_ref, c_ref, w_ref, v_ref,
-                 o_out, first_out, second_out,
-                 xa, xb, ga, gb, ha, hb, zx, zg, zh, xs, gs, hs, scratch, cube, taps,
+def block_kernel(cap, count_ref, list_ref, pos_ref, par_ref, f_ref, c_ref, w_ref, v_ref,
+                 o_out, grads_out,
+                 rows_x, rows_g, rows_h, line_x, line_g, line_h, src_x, src_g, src_h, xs, gs, hs, scratch, cube, taps,
                  taps_g, wide_g, wide_w, wide_b, wide_v, product, p_sum,
                  r1, a1, r2, r4, whole, send, recv, send_sum, recv_sum):
     g, y, x, c = place()
@@ -253,6 +262,7 @@
     ]
     zs = [device((g + k) % N_Z, y, x, c) for k in range(1, N_Z)]
     partners = [sibling] + [device(g, yy, xx, c) for yy, xx, _ in layer] + zs
+    partners += [device((g + k) % N_Z, y, x, 1 - c) for k in (1, N_Z - 1)]
     barrier = pltpu.get_barrier_semaphore()
     for partner in partners:
         pl.semaphore_signal(barrier, inc=1, device_id=partner, device_id_type=MESH)
@@ -260,9 +270,9 @@
     count = count_ref[g, lax.axis_index("dev")]
     low = lax.broadcasted_iota(jnp.int32, (1, 128), 1) < 64
     started = []
-    gx = Gather(0, (xa, xb), zx, send, recv, started)
-    gg = Gather(1, (ga, gb), zg, send, recv, started)
-    gh = Gather(2, (ha, hb), zh, send, recv, started)
+    gx = Gather(0, cap, list_ref, rows_x, line_x, src_x, send, recv, started)
+    gg = Gather(1, cap, list_ref, rows_g, line_g, src_g, send, recv, started)
+    gh = Gather(2, cap, list_ref, rows_h, line_h, src_h, send, recv, started)
 
     def live(pair):
         return jnp.where(low, 2 * pair, 2 * pair + 1) < count
@@ -285,7 +295,7 @@
         gg.write(pair, value, scratch)
 
     def forward(pair):
-        build_cube(cube, xs[pair].astype(F32), gx.bufs, pos_ref, par_ref, pair)
+        build_cube(cube, xs[pair].astype(F32), rows_x, pos_ref, par_ref, pair)
         stack_taps(cube, taps, pair)
         first = convolve(taps[pair], wide_w)
         hidden = jnp.where(live(pair), jnp.maximum(first, 0.0), 0.0)
@@ -294,14 +304,14 @@
         gh.write(pair, hidden, scratch)
 
     def backward(pair):
-        build_cube(cube, gs[pair].astype(F32), gg.bufs, pos_ref, par_ref, pair)
+        build_cube(cube, gs[pair].astype(F32), rows_g, pos_ref, par_ref, pair)
         stack_taps(cube, taps_g, 0)
         back = convolve(taps_g[0], wide_b, True)
         grad = jnp.where(hs[pair].astype(F32) > 0, back, 0.0)
         spread(wide_g, pair, grad.astype(BF16))
 
     def stack_h(pair):
-        build_cube(cube, hs[pair].astype(F32), gh.bufs, pos_ref, par_ref, pair)
+        build_cube(cube, hs[pair].astype(F32), rows_h, pos_ref, par_ref, pair)
         stack_taps(cube, taps, pair)
         spread(wide_g, pair, gs[pair])
 
@@ -314,30 +324,30 @@
 
     over_pairs(pack_x)
     pl.semaphore_wait(barrier, len(partners))
-    gx.layers()
+    gx.begin()
     over_pairs(pack_g)
-    gg.layers()
+    gg.begin()
     gx.step0()
     for one in (gx, gg, gh):
         one.clear()
     widen(w_ref, wide_w, False)
     gx.step1()
+    gg.step0()
+    gx.step2()
+    gg.step1()
     widen(v_ref, wide_b, True)
-    gx.step2()
     widen(v_ref, wide_v, False)
     wide_g[...] = jnp.zeros((PAIRS, 640, 384), BF16)
     gx.step3()
-    gg.step0()
     gx.step4()
-    gg.step1()
+    gg.step2()
     gx.step5()
     over_pairs(forward)
-    gh.layers()
-    gg.step2()
+    gh.begin()
     gh.step0()
     gh.step1()
+    gg.step3()
     gh.step2()
-    gg.step3()
     gg.step4()
     gg.step5()
     over_pairs(backward)
@@ -411,26 +421,24 @@
     copy(whole.at[half], whole.at[half], sibling).wait()
     for q in range(9):
         for tz in range(3):
-            value = whole[pl.ds((q * 3 + tz) * 64, 64)].astype(F32)
-            first_out[tz * 9 + q] = value[:, 0:64]
-            second_out[tz * 9 + q] = pltpu.roll(value, 64, 1)[:, 0:64]
+            grads_out[tz * 9 + q] = whole[pl.ds((q * 3 + tz) * 64, 64)]
     for one in started:
         one.wait_send()
 
 
-def block(counts, pos, parity, features, cotangent, w, v):
+def block(cap, collective_id, counts, lists, pos, parity, features, cotangent, w, v):
     smem, vmem = pl.BlockSpec(memory_space=pltpu.SMEM), pl.BlockSpec(memory_space=pltpu.VMEM)
     return pl.pallas_call(
-        block_kernel,
-        in_specs=[smem] * 3 + [vmem] * 4,
-        out_specs=[vmem] * 3,
+        functools.partial(block_kernel, cap),
+        in_specs=[smem] * 4 + [vmem] * 4,
+        out_specs=[vmem] * 2,
         out_shape=[
             jax.ShapeDtypeStruct((PAIRS, 128, 512), BF16),
-            jax.ShapeDtypeStruct((27, 64, 64), F32),
-            jax.ShapeDtypeStruct((27, 64, 64), F32),
+            jax.ShapeDtypeStruct((27, 64, 128), BF16),
         ],
-        scratch_shapes=[pltpu.VMEM((97, 3, 64, 128), BF16)] * 6
-        + [pltpu.VMEM((2, PAIRS, 1, 64, 128), BF16)] * 3
+        scratch_shapes=[pltpu.VMEM((2, 97, 3, 64, 128), BF16)] * 3
+        + [pltpu.VMEM((24, 3, 64, 128), BF16)] * 3
+        + [pltpu.VMEM((2, PAIRS, 3, 64, 128), BF16)] * 3
         + [pltpu.VMEM((PAIRS, 512, 128), BF16)] * 3
         + [
             pltpu.VMEM((512, 128), F32),
@@ -448,31 +456,56 @@
             pltpu.VMEM((16, 64, 128), BF16),
             pltpu.VMEM((N_Z, 64, 128), BF16),
             pltpu.VMEM((2048, 128), BF16),
-            pltpu.SemaphoreType.DMA((3, 2, 14)),
-            pltpu.SemaphoreType.DMA((3, 2, 14)),
+            pltpu.SemaphoreType.DMA((3, 16)),
+            pltpu.SemaphoreType.DMA((3, 16)),
             pltpu.SemaphoreType.DMA((40,)),
             pltpu.SemaphoreType.DMA((40,)),
         ],
         compiler_params=pltpu.CompilerParams(
-            collective_id=0, has_side_effects=True, vmem_limit_bytes=62 * 2**20
+            collective_id=collective_id, has_side_effects=True, vmem_limit_bytes=62 * 2**20
         ),
-    )(counts, pos, parity, features, cotangent, w, v)
-
-
-def halo_places(neighbours):
-    halves = jnp.asarray(np.array([face_of(d)[0] for d in DIRECTIONS], np.int32))[None, :]
+    )(counts, lists, pos, parity, features, cotangent, w, v)
+
+
+def tables(counts, neighbours):
+    d = np.arange(32)
+    row = np.stack([d // 8, d // 2 % 4]).astype(np.int32)
+    order = np.stack([d // 2 % 4 * 2 + d % 2, d // 8 * 2 + d % 2]).astype(np.int32)
+    before = (row[:, :, None] == row[:, None, :]) & (order[:, None, :] < order[:, :, None])
+    pairs = (counts + 1) // 2
+    base = jnp.sum(jnp.where(before[:, None], pairs[None, :, None, :], 0), axis=3)
+    needed = jnp.max(base + pairs[None])
+
+    halves = np.array([face_of(k)[0] for k in DIRECTIONS], np.int32)[None, :]
     dev = neighbours // 6 % 32
-    y, x, c = dev // 8, dev // 2 % 4, dev % 2
-    first = jnp.where(halves == 0, x, y)
-    second = jnp.where(halves == 0, y, x)
-    pos = ((c * 4 + second) * 4 + first) * 3 + neighbours % 6 // 2
-    return jnp.where(neighbours >= 0, pos, 96).astype(jnp.int32), neighbours % 2
+    hit = (neighbours // 6)[:, :, None] == np.arange(256, dtype=np.int32)
+    bases = jnp.where(halves[:, :, None] == 0, base[0].reshape(256), base[1].reshape(256))
+    rank = jnp.sum(jnp.where(hit, bases, 0), axis=2) + neighbours % 6 // 2
+    pos = jnp.where(halves == 0, dev // 8, dev // 2 % 4) * 24 + rank
+    pos = jnp.where(neighbours >= 0, pos, 96).astype(jnp.int32)
+
+    g, y, x, c = place()
+    own_row = jnp.where(c == 0, y, x)
+    rows, orders = jnp.where(c == 0, row[0], row[1]), jnp.where(c == 0, order[0], order[1])
+    groups = jnp.stack([g, (g + jnp.where(c == 0, 1, N_Z - 1)) % N_Z])
+    p = np.arange(3, dtype=np.int32)
+    ranks = jnp.where(c == 0, base[0], base[1])[:, :, None] + p
+    sent = (rows == own_row)[None, :, None] & (p < pairs[:, :, None])
+    here = np.arange(N_Z, dtype=np.int32)[None, :] == groups[:, None]
+    match = (
+        here[:, None, :, None, None]
+        & sent[None, None]
+        & (ranks[None, None] == np.arange(24, dtype=np.int32)[None, :, None, None, None])
+    )
+    lists = jnp.sum(jnp.where(match, (orders[:, None] * 3 + p)[None, None, None], 0), axis=(2, 3, 4))
+    return needed, lists.astype(jnp.int32), pos, neighbours % 2
 
 
 def per_device(features, cotangent, first_weight, second_weight, counts, neighbours):
-    pos, parity = halo_places(neighbours)
-    out, first_grad, second_grad = block(
+    needed, lists, pos, parity = tables(counts, neighbours)
+    operands = (
         counts,
+        lists,
         pos,
         parity,
         features.reshape(PAIRS, 128, 512),
@@ -480,10 +513,16 @@
         first_weight.transpose(1, 0, 2),
         second_weight.transpose(1, 0, 2),
     )
+    out, grads = lax.cond(
+        needed <= 16,
+        functools.partial(block, 16, 0),
+        functools.partial(block, 24, 1),
+        *operands,
+    )
     return (
         out.reshape(6, 64, 512),
-        first_grad.transpose(1, 0, 2),
-        second_grad.transpose(1, 0, 2),
+        grads[:, :, :64].astype(F32).transpose(1, 0, 2),
+        grads[:, :, 64:].astype(F32).transpose(1, 0, 2),
     )
 
 

time: 147 us -> 123 us (0.84)
  Pallas kernels: 140 us -> 113 us
  other arithmetic: 0.63 us -> 6.79 us
  local copies, waits for them, and re-layouts: 5.62 us -> 1.35 us
    pallas_call x1, Pallas kernels: 140 us -> 113 us  [block(): pl.pallas_call(functools.partial(block_kernel, cap), in_specs=[smem] * 4...]
    unnamed x9 -> x15, local copies, waits for them, and re-layouts: 5.62 us -> 1.19 us
    select_n x1 -> x4, other arithmetic: 0.63 us -> 2.86 us  [the longest x1 0.73 us: tables(): return (needed, lists.astype(jnp.int32), pos, neighbours % 2)]
    reduce_sum x0 -> x3, other arithmetic: none -> 1.55 us  [the longest x1 0.95 us: tables(): jnp.sum(jnp.where(match, (orders[:, None] * 3 + p)[None, None, None], 0),...]
where the time goes in v4:
time: 123 us
  Pallas kernels  113 us (92%)
  other arithmetic  6.79 us (6%)
  between operations  1.46 us (1%)
  local copies, waits for them, and re-layouts  1.35 us (1%)
    pallas_call x1, Pallas kernels, block(): pl.pallas_call(functools.partial(block_kernel, cap), in_specs=[smem] * 4...  113 us

profile of v4, /device:TPU:1, one launch (start us, length us, event | category | flops | bytes accessed | tf_op | source)
XLA Modules:
  0.0 122.8 jit_solution(17538709922335405945)
XLA Ops:
  0.6 0.0 copy-start.3
  0.6 0.0 copy-start.4
  0.7 0.0 copy-start.5
  0.7 0.0 copy-start.6
  0.7 0.0 copy-start.2
  0.7 0.0 copy-start
  0.8 0.1 pad_add_fusion
  0.8 0.1 iota_compare_fusion.3
  0.9 0.4 copy-done.3
  1.3 0.0 copy-done.4
  1.3 0.0 copy-done.5
  1.3 0.0 copy-done.6
  1.4 0.7 add_select_fusion.8
  2.1 0.1 broadcast_and_fusion
  2.1 0.7 add_select_fusion.7
  2.8 0.0 copy-done.2
  2.8 0.3 select_reduce_fusion.1
  3.2 0.6 add_reduce_fusion
  4.5 0.1 broadcast_in_dim.108
  4.6 0.1 broadcast_in_dim.110
  4.7 0.7 broadcast_select_fusion
  5.4 0.3 select_reduce_fusion.2
  5.6 0.7 add_select_fusion
  6.4 0.0 copy-start.1
  6.4 1.0 select_reduce_fusion
  7.4 0.0 copy-done
  7.4 0.0 copy-done.1
  7.4 113.2 %conditional.1 = (bf16[27,64,128]{2,1,0:T(8,128)(2,1)S(1)}, bf16[6,64,512]{2,1,0:T(8,128)(2,1)S(1)}) conditional(s32[]{:T(128)} %convert_element_type.2, (s32[8,32]{1,0:T(8,128)S(1)}, s32[2,24]{1,0:T(2,128)S(1)}, s32[6,26]{1,0:T(8,128)S(1)}, s32[6,26]{1,0:T(8,128)S(1)}, bf16[3,128,512]{2,1,0:T(8,128)(2,1)}, /*index=5*/bf16[3,128,512]{2,1,0:T(8,128)(2,1)}, ...), branch_computations={%region_4.5_spmd, %region_5.6_spmd} | conditional | bytes 16 | solution.py:516
  7.6 113.0 %branch_1_fun.1 = (bf16[3,128,512]{2,1,0:T(8,128)(2,1)S(1)}, bf16[27,64,128]{2,1,0:T(8,128)(2,1)S(1)}) custom-call(s32[8,32]{1,0:T(8,128)S(1)} %get-tuple-element.47.count_ref, s32[2,24]{1,0:T(2,128)S(1)} %get-tuple-element.48.list_ref, s32[6,26]{1,0:T(8,128)S(1)} %get-tuple-element.49.pos_ref, s32[6,26]{1,0:T(8,128)S(1)} %get-tuple-element.50.par_ref, ...), custom_call_target="tpu_custom_call" | custom-call | tf_op jit(solution)/shard_map/cond/branch_1_fun/pallas_call | solution.py:431
  120.6 1.4 %convert_bitcast_fusion = (f32[64,27,64]{2,0,1:T(8,128)}, f32[64,27,64]{2,0,1:T(8,128)}) fusion(bf16[27,64,128]{2,1,0:T(8,128)(2,1)S(1)} %get-tuple-element.63), kind=kLoop, calls=%fused_computation | loop fusion | flops 221184 | bytes 1327104 | tf_op jit(solution)/shard_map/transpose | solution.py:525
  122.1 0.7 copy.25
  (7 shorter events, 0.1 us)
Async XLA Ops:
  0.6 0.7 copy-start.3
  0.6 0.7 copy-start.4
  0.7 0.7 copy-start.5
  0.7 0.7 copy-start.6
  0.7 2.2 %copy-start.2 = (pred[2,32,32]{2,1,0:T(32,128)(4,1)S(1)}, pred[2,32,32]{2,1,0:T(32,128)(4,1)}, u32[]{:S(2)}) copy-start(pred[2,32,32]{2,1,0:T(32,128)(4,1)} %constant.179) | copy-start | bytes 6148
  0.7 6.7 %copy-start = (bf16[64,27,64]{2,0,1:T(8,128)(2,1)S(1)}, bf16[64,27,64]{2,0,1:T(8,128)(2,1)}, u32[]{:S(2)}) copy-start(bf16[64,27,64]{2,0,1:T(8,128)(2,1)} %param.21) | copy-start | bytes 663556
  6.4 1.0 copy-start.1

commit v5 on v4

--- a/solution.py
+++ b/solution.py
@@ -13,6 +13,7 @@
 BF16 = jnp.bfloat16
 N_Z, N_Y, N_X = 8, 4, 4
 PAIRS = 3
+CAPS = (14, 16, 24)
 DIRECTIONS = [
     (dz, dy, dx)
     for dz in (-1, 0, 1)
@@ -113,50 +114,60 @@
         self.copy(0, 0, self.src.at[1 - c, :, sides], dst, self.sibling())
         self.line[pl.ds(self.i * 6 + c * 3, 3), 0:2] = self.src[c, :, 0:2]
 
+    def both_ways(self, number, part, first):
+        lower, upper = (part + (slice(None), pl.ds(start, 32)) for start in (0, 32))
+        ref = self.line if first else self.rows
+        ahead, back = self.moved(first, 1), self.moved(first, -1)
+        self.same(number, ref.at[lower], ahead)
+        self.same(number + 1, ref.at[upper], back)
+        self.same(number + 2, ref.at[upper], ahead)
+        self.same(number + 3, ref.at[lower], back)
+
     def step0(self):
         self.came(0)
         part = self.line.at[pl.ds(0, 3), pl.ds(2, 1)]
         for core in range(2):
             self.describe(1, 1 + core, part, part, self.sibling()).wait_recv()
-        for number, step in ((3, 1), (4, -1)):
-            self.same(number, self.line.at[self.block(0)], self.moved(True, step))
+        self.both_ways(3, (self.block(0),), True)
 
     def step1(self):
-        for number, step, rows in ((5, 1, pl.ds(0, 32)), (6, -1, pl.ds(32, 32))):
-            self.came(number - 2)
-            part = self.line.at[self.block(-step), :, rows]
+        for number, step, start in ((7, 1, 0), (8, -1, 32)):
+            self.came(number - 4)
+            part = self.line.at[self.block(-step), :, pl.ds(start, 32)]
             self.same(number, part, self.moved(True, step))
 
     def step2(self):
-        self.came(5, 6)
+        self.came(5, 6, 7, 8)
 
         def one(k, carry):
             at = self.j * 24 + k
-            self.rows[self.c, at, 0:2] = self.line[self.list_ref[0, k], 0:2]
-            self.rows[self.c, at, 2:3] = self.line[self.list_ref[1, k], 2:3]
+            self.rows[self.c, at, 0:2] = self.line[self.list_ref[k, 0], 0:2]
+            self.rows[self.c, at, 2:3] = self.line[self.list_ref[k, 1], 2:3]
             return carry
 
         lax.fori_loop(0, self.cap, one, 0)
-        part = self.rows.at[self.c, self.row(0)]
-        for number, step in ((7, 1), (8, -1)):
+        self.both_ways(9, (self.c, self.row(0)), False)
+        self.same(15, self.rows.at[self.c, self.row(0)], self.sibling())
+
+    def step3(self):
+        for number, step, start in ((13, 1, 0), (14, -1, 32)):
+            self.came(number - 4)
+            part = self.rows.at[self.c, self.row(-step), :, pl.ds(start, 32)]
             self.same(number, part, self.moved(False, step))
-        self.same(11, part, self.sibling())
-
-    def step3(self):
-        for number, step, rows in ((9, 1, pl.ds(0, 32)), (10, -1, pl.ds(32, 32))):
-            self.came(number - 2)
-            part = self.rows.at[self.c, self.row(-step), :, rows]
-            self.same(number, part, self.moved(False, step))
-            self.same(number + 3, self.rows.at[self.c, self.row(-step)], self.sibling())
 
     def step4(self):
-        for number, rows in ((9, pl.ds(0, 32)), (10, pl.ds(32, 32))):
+        for number, step in ((16, 1), (17, -1)):
+            self.came(number - 5)
+            self.same(number, self.rows.at[self.c, self.row(-step)], self.sibling())
+
+    def step5(self):
+        for number, start in ((13, 0), (14, 32)):
             self.came(number)
-            part = self.rows.at[self.c, self.row(2), :, rows]
+            part = self.rows.at[self.c, self.row(2), :, pl.ds(start, 32)]
             self.same(number + 5, part, self.sibling())
 
-    def step5(self):
-        self.came(11, 12, 13, 14, 15)
+    def step6(self):
+        self.came(15, 16, 17, 18, 19)
 
 
 def build_cube(cube, own, rows_ref, pos_ref, par_ref, pair):
@@ -325,33 +336,36 @@
     over_pairs(pack_x)
     pl.semaphore_wait(barrier, len(partners))
     gx.begin()
-    over_pairs(pack_g)
-    gg.begin()
-    gx.step0()
     for one in (gx, gg, gh):
         one.clear()
+    gx.step0()
+    over_pairs(pack_g)
+    gx.step1()
+    gg.begin()
     widen(w_ref, wide_w, False)
-    gx.step1()
+    gx.step2()
     gg.step0()
-    gx.step2()
+    widen(v_ref, wide_b, True)
+    gx.step3()
     gg.step1()
-    widen(v_ref, wide_b, True)
     widen(v_ref, wide_v, False)
     wide_g[...] = jnp.zeros((PAIRS, 640, 384), BF16)
-    gx.step3()
     gx.step4()
+    gx.step5()
     gg.step2()
-    gx.step5()
+    gx.step6()
     over_pairs(forward)
     gh.begin()
+    gg.step3()
     gh.step0()
     gh.step1()
-    gg.step3()
+    gg.step4()
     gh.step2()
-    gg.step4()
     gg.step5()
+    gg.step6()
     over_pairs(backward)
     gh.step3()
+    gh.step4()
     product[...] = outer(wide_g, taps)
     for q in range(9):
         for tz in range(3):
@@ -360,8 +374,8 @@
             one = product[even, lanes] + pltpu.roll(product[odd, lanes], 64, 1)
             p_sum[pl.ds((q * 3 + tz) * 64, 64), :] = one
     p_sum[1728:2048, :] = jnp.zeros((320, 128), F32)
-    gh.step4()
     gh.step5()
+    gh.step6()
     over_pairs(stack_h)
     product[...] = outer(wide_g, taps)
     for q in range(9):
@@ -456,8 +470,8 @@
             pltpu.VMEM((16, 64, 128), BF16),
             pltpu.VMEM((N_Z, 64, 128), BF16),
             pltpu.VMEM((2048, 128), BF16),
-            pltpu.SemaphoreType.DMA((3, 16)),
-            pltpu.SemaphoreType.DMA((3, 16)),
+            pltpu.SemaphoreType.DMA((3, 20)),
+            pltpu.SemaphoreType.DMA((3, 20)),
             pltpu.SemaphoreType.DMA((40,)),
             pltpu.SemaphoreType.DMA((40,)),
         ],
@@ -467,38 +481,73 @@
     )(counts, lists, pos, parity, features, cotangent, w, v)
 
 
+def table_kernel(counts_ref, near_ref, needed_out, list_out, pos_out, par_out):
+    g, y, x, c = place()
+    iota = lambda shape, dim: lax.broadcasted_iota(jnp.int32, shape, dim)
+    rows = (lambda d: d >> 3, lambda d: (d >> 1) & 3)
+    orders = (lambda d: (d >> 1 & 3) * 2 + (d & 1), lambda d: (d >> 3) * 2 + (d & 1))
+    pairs = ((counts_ref[...] + 1) >> 1).astype(F32)
+    other, this = iota((32, 32), 0), iota((32, 32), 1)
+    base = []
+    for half in range(2):
+        before = (rows[half](other) == rows[half](this)) & (
+            orders[half](other) < orders[half](this)
+        )
+        base.append(jnp.dot(pairs, before.astype(F32), preferred_element_type=F32))
+    top = jnp.max(jnp.maximum(base[0], base[1]) + pairs)
+    needed_out[0] = top.astype(jnp.int32)
+
+    group = iota((N_Z, 32), 0)
+
+    def of_group(value, which):
+        return jnp.sum(jnp.where(group == which, value, 0.0), axis=0, keepdims=True)
+
+    near = near_ref[...]
+    owner = (near * 10923) >> 16
+    within = near - 6 * owner
+    dev = owner & 31
+    lane, device_lane = iota((6, 26), 1), iota((6, 32), 1)
+    pos = jnp.zeros((6, 26), jnp.int32)
+    for k, direction in enumerate(DIRECTIONS):
+        half = face_of(direction)[0]
+        line = of_group(base[half], g + direction[0])
+        hit = dev[:, k:k + 1] == device_lane
+        rank = jnp.sum(jnp.where(hit, line, 0.0), axis=1, keepdims=True).astype(jnp.int32)
+        pos = jnp.where(lane == k, rank + rows[half](dev) * 24, pos)
+    pos_out[...] = jnp.where(near >= 0, pos + (within >> 1), 96)
+    par_out[...] = within & 1
+
+    lead = c == 0
+    d = iota((24, 32), 1)
+    own_row = jnp.where(lead, y, x)
+    inside = jnp.where(lead, rows[0](d), rows[1](d)) == own_row
+    order = jnp.where(lead, orders[0](d), orders[1](d))
+    start = jnp.where(lead, base[0], base[1])
+    for source, which in enumerate((g, (g + jnp.where(lead, 1, N_Z - 1)) % N_Z)):
+        rank = of_group(start, which).astype(jnp.int32)
+        size = of_group(pairs, which).astype(jnp.int32)
+        found = jnp.zeros((24, 1), F32)
+        for p in range(3):
+            match = inside & (rank + p == iota((24, 32), 0)) & (size > p)
+            found += jnp.sum(
+                jnp.where(match, (order * 3 + p).astype(F32), 0.0), axis=1, keepdims=True
+            )
+        list_out[:, source:source + 1] = found.astype(jnp.int32)
+
+
 def tables(counts, neighbours):
-    d = np.arange(32)
-    row = np.stack([d // 8, d // 2 % 4]).astype(np.int32)
-    order = np.stack([d // 2 % 4 * 2 + d % 2, d // 8 * 2 + d % 2]).astype(np.int32)
-    before = (row[:, :, None] == row[:, None, :]) & (order[:, None, :] < order[:, :, None])
-    pairs = (counts + 1) // 2
-    base = jnp.sum(jnp.where(before[:, None], pairs[None, :, None, :], 0), axis=3)
-    needed = jnp.max(base + pairs[None])
-
-    halves = np.array([face_of(k)[0] for k in DIRECTIONS], np.int32)[None, :]
-    dev = neighbours // 6 % 32
-    hit = (neighbours // 6)[:, :, None] == np.arange(256, dtype=np.int32)
-    bases = jnp.where(halves[:, :, None] == 0, base[0].reshape(256), base[1].reshape(256))
-    rank = jnp.sum(jnp.where(hit, bases, 0), axis=2) + neighbours % 6 // 2
-    pos = jnp.where(halves == 0, dev // 8, dev // 2 % 4) * 24 + rank
-    pos = jnp.where(neighbours >= 0, pos, 96).astype(jnp.int32)
-
-    g, y, x, c = place()
-    own_row = jnp.where(c == 0, y, x)
-    rows, orders = jnp.where(c == 0, row[0], row[1]), jnp.where(c == 0, order[0], order[1])
-    groups = jnp.stack([g, (g + jnp.where(c == 0, 1, N_Z - 1)) % N_Z])
-    p = np.arange(3, dtype=np.int32)
-    ranks = jnp.where(c == 0, base[0], base[1])[:, :, None] + p
-    sent = (rows == own_row)[None, :, None] & (p < pairs[:, :, None])
-    here = np.arange(N_Z, dtype=np.int32)[None, :] == groups[:, None]
-    match = (
-        here[:, None, :, None, None]
-        & sent[None, None]
-        & (ranks[None, None] == np.arange(24, dtype=np.int32)[None, :, None, None, None])
-    )
-    lists = jnp.sum(jnp.where(match, (orders[:, None] * 3 + p)[None, None, None], 0), axis=(2, 3, 4))
-    return needed, lists.astype(jnp.int32), pos, neighbours % 2
+    vmem = pl.BlockSpec(memory_space=pltpu.VMEM)
+    return pl.pallas_call(
+        table_kernel,
+        in_specs=[vmem] * 2,
+        out_specs=[pl.BlockSpec(memory_space=pltpu.SMEM)] + [vmem] * 3,
+        out_shape=[
+            jax.ShapeDtypeStruct((1,), jnp.int32),
+            jax.ShapeDtypeStruct((24, 2), jnp.int32),
+            jax.ShapeDtypeStruct((6, 26), jnp.int32),
+            jax.ShapeDtypeStruct((6, 26), jnp.int32),
+        ],
+    )(counts, neighbours)
 
 
 def per_device(features, cotangent, first_weight, second_weight, counts, neighbours):
@@ -513,10 +562,9 @@
         first_weight.transpose(1, 0, 2),
         second_weight.transpose(1, 0, 2),
     )
-    out, grads = lax.cond(
-        needed <= 16,
-        functools.partial(block, 16, 0),
-        functools.partial(block, 24, 1),
+    out, grads = lax.switch(
+        sum((needed[0] > cap).astype(jnp.int32) for cap in CAPS[:-1]),
+        [functools.partial(block, cap, i) for i, cap in enumerate(CAPS)],
         *operands,
     )
     return (

time: 123 us -> 111 us (0.902)
  Pallas kernels: 113 us -> 105 us
  other arithmetic: 6.79 us -> 1.43 us
    pallas_call x1, Pallas kernels: 113 us -> 104 us  [block(): pl.pallas_call(functools.partial(block_kernel, cap), in_specs=[smem] * 4...]
    select_n x4 -> x0, other arithmetic: 2.86 us -> none  [the longest x1 0.73 us: tables(): return (needed, lists.astype(jnp.int32), pos, neighbours % 2)]
    reduce_sum x3 -> x0, other arithmetic: 1.55 us -> none  [the longest x1 0.95 us: tables(): jnp.sum(jnp.where(match, (orders[:, None] * 3 + p)[None, None, None], 0),...]
    pallas_call x0 -> x1, Pallas kernels: none -> 1.47 us  [tables(): pl.pallas_call(table_kernel, in_specs=[vmem] * 2, out_specs=[pl.BlockSpec...]
where the time goes in v5:
time: 111 us; the launch traced here: 110 us
  Pallas kernels  105 us (95%)
  between operations  1.95 us (2%)
  local copies, waits for them, and re-layouts  1.43 us (1%)
  other arithmetic  1.43 us (1%)
    pallas_call x1, Pallas kernels, block(): pl.pallas_call(functools.partial(block_kernel, cap), in_specs=[smem] * 4...  104 us

profile of v5, /device:TPU:1, one launch (start us, length us, event | category | flops | bytes accessed | tf_op | source)
XLA Modules:
  0.0 110.5 jit_solution(129630041194291089)
XLA Ops:
  0.6 0.0 copy-start
  0.6 0.7 copy-done
  1.3 1.5 %shard_map.85 = (s32[1]{0:T(128)}, s32[24,2]{1,0:T(8,128)S(1)}, s32[6,26]{1,0:T(8,128)S(1)}, s32[6,26]{1,0:T(8,128)S(1)}) custom-call(s32[8,32]{1,0:T(8,128)S(1)} %copy-done, s32[6,26]{1,0:T(8,128)} %near_ref.1), custom_call_target="tpu_custom_call" | custom-call | tf_op jit(solution)/shard_map/pallas_call | solution.py:540
  4.1 104.2 %conditional.1 = (bf16[27,64,128]{2,1,0:T(8,128)(2,1)S(1)}, bf16[6,64,512]{2,1,0:T(8,128)(2,1)S(1)}) conditional(s32[]{:T(128)} %bitcast.3, (s32[8,32]{1,0:T(8,128)S(1)}, s32[24,2]{1,0:T(8,128)S(1)}, s32[6,26]{1,0:T(8,128)S(1)}, s32[6,26]{1,0:T(8,128)S(1)}, bf16[3,128,512]{2,1,0:T(8,128)(2,1)}, ...), branch_computations={%region_0.0_spmd, %region_1.0_spmd, %region_2.0_spmd} | conditional | bytes 16 | solution.py:565
  4.1 104.0 %branch_0_fun.1 = (bf16[3,128,512]{2,1,0:T(8,128)(2,1)S(1)}, bf16[27,64,128]{2,1,0:T(8,128)(2,1)S(1)}) custom-call(s32[8,32]{1,0:T(8,128)S(1)} %get-tuple-element.55.count_ref, s32[24,2]{1,0:T(8,128)S(1)} %get-tuple-element.56.list_ref, s32[6,26]{1,0:T(8,128)S(1)} %get-tuple-element.57.pos_ref, s32[6,26]{1,0:T(8,128)S(1)} %get-tuple-element.58.par_ref, ...), custom_call_target="tpu_custom_call" | custom-call | tf_op jit(solution)/shard_map/cond/branch_0_fun/pallas_call | solution.py:445
  108.3 1.4 %convert_bitcast_fusion = (f32[64,27,64]{2,0,1:T(8,128)}, f32[64,27,64]{2,0,1:T(8,128)}) fusion(bf16[27,64,128]{2,1,0:T(8,128)(2,1)S(1)} %get-tuple-element.99), kind=kLoop, calls=%fused_computation | loop fusion | flops 221184 | bytes 1327104 | tf_op jit(solution)/shard_map/transpose | solution.py:573
  109.7 0.7 copy.16
Async XLA Ops:
  0.6 0.7 copy-start

commit v6 on v5

--- a/solution.py
+++ b/solution.py
@@ -249,10 +249,10 @@
         wide_g[pair, tz * 64:tz * 64 + 512, tz * 128:tz * 128 + 128] = value
 
 
-def outer(wide_g, taps):
+def outer(one, other):
     return lax.dot_general(
-        wide_g[...].reshape(PAIRS * 640, 384),
-        taps[...].reshape(PAIRS * 640, 1152),
+        one[...].reshape(PAIRS * 640, one.shape[2]),
+        other[...].reshape(PAIRS * 640, other.shape[2]),
         (((0,), (0,)), ((), ())),
         preferred_element_type=F32,
     )
@@ -261,7 +261,7 @@
 def block_kernel(cap, count_ref, list_ref, pos_ref, par_ref, f_ref, c_ref, w_ref, v_ref,
                  o_out, grads_out,
                  rows_x, rows_g, rows_h, line_x, line_g, line_h, src_x, src_g, src_h, xs, gs, hs, scratch, cube, taps,
-                 taps_g, wide_g, wide_w, wide_b, wide_v, product, p_sum,
+                 taps_g, wide_g, wide_w, wide_b, wide_v, product, product_g, p_sum,
                  r1, a1, r2, r4, whole, send, recv, send_sum, recv_sum):
     g, y, x, c = place()
     sibling = device(g, y, x, 1 - c)
@@ -316,17 +316,14 @@
 
     def backward(pair):
         build_cube(cube, gs[pair].astype(F32), rows_g, pos_ref, par_ref, pair)
-        stack_taps(cube, taps_g, 0)
-        back = convolve(taps_g[0], wide_b, True)
+        stack_taps(cube, taps_g, pair)
+        back = convolve(taps_g[pair], wide_b, True)
         grad = jnp.where(hs[pair].astype(F32) > 0, back, 0.0)
         spread(wide_g, pair, grad.astype(BF16))
 
-    def stack_h(pair):
+    def finish(pair):
         build_cube(cube, hs[pair].astype(F32), rows_h, pos_ref, par_ref, pair)
         stack_taps(cube, taps, pair)
-        spread(wide_g, pair, gs[pair])
-
-    def finish(pair):
         second = convolve(taps[pair], wide_v)
         lane = lax.broadcasted_iota(jnp.int32, (128, 1), 0)
         slot = jnp.where(lane < 64, 2 * pair, 2 * pair + 1)
@@ -360,13 +357,13 @@
     gh.step0()
     gh.step1()
     gg.step4()
+    gg.step5()
     gh.step2()
-    gg.step5()
     gg.step6()
     over_pairs(backward)
     gh.step3()
+    product[...] = outer(wide_g, taps)
     gh.step4()
-    product[...] = outer(wide_g, taps)
     for q in range(9):
         for tz in range(3):
             even, odd = pl.ds(tz * 128, 64), pl.ds(tz * 128 + 64, 64)
@@ -374,16 +371,14 @@
             one = product[even, lanes] + pltpu.roll(product[odd, lanes], 64, 1)
             p_sum[pl.ds((q * 3 + tz) * 64, 64), :] = one
     p_sum[1728:2048, :] = jnp.zeros((320, 128), F32)
-    gh.step5()
-    gh.step6()
-    over_pairs(stack_h)
-    product[...] = outer(wide_g, taps)
+    over_pairs(lambda pair: spread(wide_g, pair, hs[pair]))
+    product_g[...] = outer(taps_g, wide_g)
     for q in range(9):
         for tz in range(3):
-            even, odd = pl.ds(tz * 128, 64), pl.ds(tz * 128 + 64, 64)
-            lanes = pl.ds(q * 128, 128)
+            even, odd = pl.ds((8 - q) * 128, 64), pl.ds((8 - q) * 128 + 64, 64)
+            lanes = pl.ds((2 - tz) * 128, 128)
             rows = pl.ds((q * 3 + tz) * 64, 64)
-            two = pltpu.roll(product[even, lanes], 64, 1) + product[odd, lanes]
+            two = pltpu.roll(product_g[even, lanes], 64, 1) + product_g[odd, lanes]
             p_sum[rows, :] = jnp.where(low, p_sum[rows, :], two)
 
     used = [0]
@@ -399,7 +394,7 @@
         return one
 
     one = copy(p_sum.at[pl.ds((1 - c) * 1024, 1024)], r1, sibling)
-    finish(0)
+    gh.step5()
     one.wait()
     a1[...] = (p_sum[pl.ds(c * 1024, 1024)] + r1[...]).astype(BF16)
 
@@ -407,7 +402,8 @@
         copy(a1.at[pl.ds((yy * N_X + xx) * 64, 64)], r2.at[k], device(g, yy, xx, c))
         for yy, xx, k in layer
     ]
-    finish(1)
+    gh.step6()
+    finish(0)
     for one in made:
         one.wait()
     at = y * N_X + x
@@ -417,7 +413,7 @@
     r4[g] = part.astype(BF16)
 
     made = [copy(r4.at[g], r4.at[g], target) for target in zs]
-    finish(2)
+    finish(1)
     for one in made:
         one.wait()
     part = r4[0].astype(F32)
@@ -429,6 +425,7 @@
     made = [
         copy(whole.at[rows], whole.at[rows], device(g, yy, xx, c)) for yy, xx, _ in layer
     ]
+    finish(2)
     for one in made:
         one.wait()
     half = pl.ds(c * 1024, 1024)
@@ -458,12 +455,13 @@
             pltpu.VMEM((512, 128), F32),
             pltpu.VMEM((10, 10, 24, 128), F32),
             pltpu.VMEM((PAIRS, 640, 1152), BF16),
-            pltpu.VMEM((1, 640, 1152), BF16),
+            pltpu.VMEM((PAIRS, 640, 1152), BF16),
             pltpu.VMEM((PAIRS, 640, 384), BF16),
             pltpu.VMEM((384, 1152), BF16),
             pltpu.VMEM((1152, 384), BF16),
             pltpu.VMEM((384, 1152), BF16),
             pltpu.VMEM((384, 1152), F32),
+            pltpu.VMEM((1152, 384), F32),
             pltpu.VMEM((2048, 128), F32),
             pltpu.VMEM((1024, 128), F32),
             pltpu.VMEM((1024, 128), BF16),

time: 111 us -> 106 us (0.955)
  Pallas kernels: 105 us -> 100 us
    pallas_call x1, Pallas kernels: 104 us -> 98.9 us  [block(): pl.pallas_call(functools.partial(block_kernel, cap), in_specs=[smem] * 4...]
where the time goes in v6:
time: 106 us; the launch traced here: 105 us
  Pallas kernels  100 us (94%)
  between operations  1.95 us (2%)
  local copies, waits for them, and re-layouts  1.43 us (1%)
  other arithmetic  1.43 us (1%)
    pallas_call x1, Pallas kernels, block(): pl.pallas_call(functools.partial(block_kernel, cap), in_specs=[smem] * 4...  98.9 us

profile of v6, /device:TPU:1, one launch (start us, length us, event | category | flops | bytes accessed | tf_op | source)
XLA Modules:
  0.0 105.5 jit_solution(12044455073662060441)
XLA Ops:
  0.6 0.0 copy-start
  0.6 0.7 copy-done
  1.3 1.5 %shard_map.85 = (s32[1]{0:T(128)}, s32[24,2]{1,0:T(8,128)S(1)}, s32[6,26]{1,0:T(8,128)S(1)}, s32[6,26]{1,0:T(8,128)S(1)}) custom-call(s32[8,32]{1,0:T(8,128)S(1)} %copy-done, s32[6,26]{1,0:T(8,128)} %near_ref.1), custom_call_target="tpu_custom_call" | custom-call | tf_op jit(solution)/shard_map/pallas_call | solution.py:538
  4.1 99.2 %conditional.1 = (bf16[27,64,128]{2,1,0:T(8,128)(2,1)S(1)}, bf16[6,64,512]{2,1,0:T(8,128)(2,1)S(1)}) conditional(s32[]{:T(128)} %bitcast.3, (s32[8,32]{1,0:T(8,128)S(1)}, s32[24,2]{1,0:T(8,128)S(1)}, s32[6,26]{1,0:T(8,128)S(1)}, s32[6,26]{1,0:T(8,128)S(1)}, bf16[3,128,512]{2,1,0:T(8,128)(2,1)}, ...), branch_computations={%region_0.0_spmd, %region_1.0_spmd, %region_2.0_spmd} | conditional | bytes 16 | solution.py:563
  4.1 98.9 %branch_0_fun.1 = (bf16[3,128,512]{2,1,0:T(8,128)(2,1)S(1)}, bf16[27,64,128]{2,1,0:T(8,128)(2,1)S(1)}) custom-call(s32[8,32]{1,0:T(8,128)S(1)} %get-tuple-element.55.count_ref, s32[24,2]{1,0:T(8,128)S(1)} %get-tuple-element.56.list_ref, s32[6,26]{1,0:T(8,128)S(1)} %get-tuple-element.57.pos_ref, s32[6,26]{1,0:T(8,128)S(1)} %get-tuple-element.58.par_ref, ...), custom_call_target="tpu_custom_call" | custom-call | tf_op jit(solution)/shard_map/cond/branch_0_fun/pallas_call | solution.py:442
  103.3 1.4 %convert_bitcast_fusion = (f32[64,27,64]{2,0,1:T(8,128)}, f32[64,27,64]{2,0,1:T(8,128)}) fusion(bf16[27,64,128]{2,1,0:T(8,128)(2,1)S(1)} %get-tuple-element.99), kind=kLoop, calls=%fused_computation | loop fusion | flops 221184 | bytes 1327104 | tf_op jit(solution)/shard_map/transpose | solution.py:571
  104.7 0.7 copy.16
Async XLA Ops:
  0.6 0.7 copy-start

commit v7 on v6

--- a/solution.py
+++ b/solution.py
@@ -271,7 +271,8 @@
         for kx in range(N_X)
         if (ky, kx) != (0, 0)
     ]
-    zs = [device((g + k) % N_Z, y, x, c) for k in range(1, N_Z)]
+    layer.sort(key=lambda to: -sum(min(k, 4 - k) for k in divmod(to[2], N_X)))
+    zs = [device((g + k) % N_Z, y, x, c) for k in (4, 3, 5, 2, 6, 1, 7)]
     partners = [sibling] + [device(g, yy, xx, c) for yy, xx, _ in layer] + zs
     partners += [device((g + k) % N_Z, y, x, 1 - c) for k in (1, N_Z - 1)]
     barrier = pltpu.get_barrier_semaphore()
@@ -425,11 +426,16 @@
     made = [
         copy(whole.at[rows], whole.at[rows], device(g, yy, xx, c)) for yy, xx, _ in layer
     ]
+    passed = [copy(whole.at[rows], whole.at[rows], sibling)]
     finish(2)
-    for one in made:
+    for one, (_, _, k) in zip(made, layer):
         one.wait()
-    half = pl.ds(c * 1024, 1024)
-    copy(whole.at[half], whole.at[half], sibling).wait()
+        ky, kx = divmod(k, N_X)
+        origin = (y - ky + N_Y) % N_Y * N_X + (x - kx + N_X) % N_X
+        part = whole.at[pl.ds(c * 1024 + origin * 64, 64)]
+        passed.append(copy(part, part, sibling))
+    for one in passed:
+        one.wait()
     for q in range(9):
         for tz in range(3):
             grads_out[tz * 9 + q] = whole[pl.ds((q * 3 + tz) * 64, 64)]
@@ -470,8 +476,8 @@
             pltpu.VMEM((2048, 128), BF16),
             pltpu.SemaphoreType.DMA((3, 20)),
             pltpu.SemaphoreType.DMA((3, 20)),
-            pltpu.SemaphoreType.DMA((40,)),
-            pltpu.SemaphoreType.DMA((40,)),
+            pltpu.SemaphoreType.DMA((56,)),
+            pltpu.SemaphoreType.DMA((56,)),
         ],
         compiler_params=pltpu.CompilerParams(
             collective_id=collective_id, has_side_effects=True, vmem_limit_bytes=62 * 2**20

time: 106 us -> 104 us (0.981)
  Pallas kernels: 100 us -> 98.3 us
    pallas_call x1, Pallas kernels: 98.9 us -> 96.8 us  [block(): pl.pallas_call(functools.partial(block_kernel, cap), in_specs=[smem] * 4...]
where the time goes in v7:
time: 104 us; the launch traced here: 103 us
  Pallas kernels  98.3 us (95%)
  between operations  1.95 us (2%)
  local copies, waits for them, and re-layouts  1.43 us (1%)
  other arithmetic  1.43 us (1%)
    pallas_call x1, Pallas kernels, block(): pl.pallas_call(functools.partial(block_kernel, cap), in_specs=[smem] * 4...  96.8 us

profile of v7, /device:TPU:1, one launch (start us, length us, event | category | flops | bytes accessed | tf_op | source)
XLA Modules:
  0.0 103.4 jit_solution(16437201134370971079)
XLA Ops:
  0.6 0.0 copy-start
  0.6 0.7 copy-done
  1.3 1.5 %shard_map.85 = (s32[1]{0:T(128)}, s32[24,2]{1,0:T(8,128)S(1)}, s32[6,26]{1,0:T(8,128)S(1)}, s32[6,26]{1,0:T(8,128)S(1)}) custom-call(s32[8,32]{1,0:T(8,128)S(1)} %copy-done, s32[6,26]{1,0:T(8,128)} %near_ref.1), custom_call_target="tpu_custom_call" | custom-call | tf_op jit(solution)/shard_map/pallas_call | solution.py:544
  4.1 97.1 %conditional.1 = (bf16[27,64,128]{2,1,0:T(8,128)(2,1)S(1)}, bf16[6,64,512]{2,1,0:T(8,128)(2,1)S(1)}) conditional(s32[]{:T(128)} %bitcast.3, (s32[8,32]{1,0:T(8,128)S(1)}, s32[24,2]{1,0:T(8,128)S(1)}, s32[6,26]{1,0:T(8,128)S(1)}, s32[6,26]{1,0:T(8,128)S(1)}, bf16[3,128,512]{2,1,0:T(8,128)(2,1)}, ...), branch_computations={%region_0.0_spmd, %region_1.0_spmd, %region_2.0_spmd} | conditional | bytes 16 | solution.py:569
  4.1 96.8 %branch_0_fun.1 = (bf16[3,128,512]{2,1,0:T(8,128)(2,1)S(1)}, bf16[27,64,128]{2,1,0:T(8,128)(2,1)S(1)}) custom-call(s32[8,32]{1,0:T(8,128)S(1)} %get-tuple-element.55.count_ref, s32[24,2]{1,0:T(8,128)S(1)} %get-tuple-element.56.list_ref, s32[6,26]{1,0:T(8,128)S(1)} %get-tuple-element.57.pos_ref, s32[6,26]{1,0:T(8,128)S(1)} %get-tuple-element.58.par_ref, ...), custom_call_target="tpu_custom_call" | custom-call | tf_op jit(solution)/shard_map/cond/branch_0_fun/pallas_call | solution.py:448
  101.2 1.4 %convert_bitcast_fusion = (f32[64,27,64]{2,0,1:T(8,128)}, f32[64,27,64]{2,0,1:T(8,128)}) fusion(bf16[27,64,128]{2,1,0:T(8,128)(2,1)S(1)} %get-tuple-element.99), kind=kLoop, calls=%fused_computation | loop fusion | flops 221184 | bytes 1327104 | tf_op jit(solution)/shard_map/transpose | solution.py:577
  102.6 0.7 copy.16
Async XLA Ops:
  0.6 0.7 copy-start

commit v8 on v7

--- a/solution.py
+++ b/solution.py
@@ -358,8 +358,8 @@
     gh.step0()
     gh.step1()
     gg.step4()
+    gh.step2()
     gg.step5()
-    gh.step2()
     gg.step6()
     over_pairs(backward)
     gh.step3()

time: 104 us -> 103 us (level)
  no operation moved by 1% of the time
where the time goes in v8:
time: 103 us
  Pallas kernels  97.8 us (95%)
  between operations  1.95 us (2%)
  local copies, waits for them, and re-layouts  1.43 us (1%)
  other arithmetic  1.43 us (1%)
    pallas_call x1, Pallas kernels, block(): pl.pallas_call(functools.partial(block_kernel, cap), in_specs=[smem] * 4...  96.3 us

profile of v8, /device:TPU:1, one launch (start us, length us, event | category | flops | bytes accessed | tf_op | source)
XLA Modules:
  0.0 102.9 jit_solution(5268100740295851658)
XLA Ops:
  0.6 0.0 copy-start
  0.6 0.7 copy-done
  1.3 1.5 %shard_map.85 = (s32[1]{0:T(128)}, s32[24,2]{1,0:T(8,128)S(1)}, s32[6,26]{1,0:T(8,128)S(1)}, s32[6,26]{1,0:T(8,128)S(1)}) custom-call(s32[8,32]{1,0:T(8,128)S(1)} %copy-done, s32[6,26]{1,0:T(8,128)} %near_ref.1), custom_call_target="tpu_custom_call" | custom-call | tf_op jit(solution)/shard_map/pallas_call | solution.py:544
  4.1 96.6 %conditional.1 = (bf16[27,64,128]{2,1,0:T(8,128)(2,1)S(1)}, bf16[6,64,512]{2,1,0:T(8,128)(2,1)S(1)}) conditional(s32[]{:T(128)} %bitcast.3, (s32[8,32]{1,0:T(8,128)S(1)}, s32[24,2]{1,0:T(8,128)S(1)}, s32[6,26]{1,0:T(8,128)S(1)}, s32[6,26]{1,0:T(8,128)S(1)}, bf16[3,128,512]{2,1,0:T(8,128)(2,1)}, ...), branch_computations={%region_0.0_spmd, %region_1.0_spmd, %region_2.0_spmd} | conditional | bytes 16 | solution.py:569
  4.1 96.3 %branch_0_fun.1 = (bf16[3,128,512]{2,1,0:T(8,128)(2,1)S(1)}, bf16[27,64,128]{2,1,0:T(8,128)(2,1)S(1)}) custom-call(s32[8,32]{1,0:T(8,128)S(1)} %get-tuple-element.55.count_ref, s32[24,2]{1,0:T(8,128)S(1)} %get-tuple-element.56.list_ref, s32[6,26]{1,0:T(8,128)S(1)} %get-tuple-element.57.pos_ref, s32[6,26]{1,0:T(8,128)S(1)} %get-tuple-element.58.par_ref, ...), custom_call_target="tpu_custom_call" | custom-call | tf_op jit(solution)/shard_map/cond/branch_0_fun/pallas_call | solution.py:448
  100.7 1.4 %convert_bitcast_fusion = (f32[64,27,64]{2,0,1:T(8,128)}, f32[64,27,64]{2,0,1:T(8,128)}) fusion(bf16[27,64,128]{2,1,0:T(8,128)(2,1)S(1)} %get-tuple-element.99), kind=kLoop, calls=%fused_computation | loop fusion | flops 221184 | bytes 1327104 | tf_op jit(solution)/shard_map/transpose | solution.py:577
  102.1 0.7 copy.16
Async XLA Ops:
  0.6 0.7 copy-start
